TPU v7x, 32 devices: a whole 2x2x4 slice. The times are simulated.
32 devices in a mesh: energy: 4 (over x, core), atom: 8 (over z, y).
Axes of the slice: x: 2, y: 2, z: 4, core: 2. Of those that a mesh axis runs over, the one named last changes fastest.
Arguments:
- green: bfloat16 [32, 2, 12, 12, 512], P('atom', None, None, None, 'energy'), may hold values from -6 to 6
- coupling: bfloat16 [32, 10368], P('atom'), may hold values from -0.375 to 0.375
- neighbours: int32 [32, 24], P('atom'), may hold values from 0 to 31, as said below
- shifts: int32 [16], replicated, may hold values from 1 to 64, as said below
- weights: float32 [16], replicated, may hold values from 0.1 to 1
Outputs:
- self_energy: bfloat16 [32, 2, 12, 12, 512], P('atom', None, None, None, 'energy')
Inputs may be any that keep to these rules, and one draw needn't show every extreme that they name: `neighbours`: of the 24 x 4 entries in the rows of one device's atoms, exactly 12 name atoms held by other devices, at most 2 of them atoms of any one device, and in every draw some device's entries reach 2 for some other device; the other remote entries are spread evenly over the remaining devices. `shifts`: one of them equals 64.
All inputs are finite; a program needn't handle non-finite values.
Results may differ from a plain program's by a relative error of at most 0.012.
Values may be sent and summed in bfloat16 or wider, within the bound.
No kernel may reach another device: no remote copies, remote signals or barrier semaphores. Data moves between devices by JAX's collectives and lax.ppermute only.
A program may use at most 128 MiB of HBM per device.

v0:
```python
import jax
import jax.numpy as jnp
from jax import lax
from jax.sharding import PartitionSpec as P

ORB = 12
NBR = 24
DIRS = 3
MAXS = 64
CAP = 2


def from_behind(value, axis, by):
    peers = lax.axis_size(axis)
    pairs = [(i, i + by) for i in range(peers) if 0 <= i + by < peers]
    return lax.ppermute(value, axis, pairs)


def band_kernel(shifts, weights, span_in, span_out):
    source = jnp.arange(span_in, dtype=jnp.int32)
    target = jnp.arange(span_out, dtype=jnp.int32)
    hits = (source[None, :, None] == target[None, None, :] + shifts[:, None, None]).astype(
        jnp.float32
    )
    band = jnp.sum(hits * weights[:, None, None], axis=0)
    kernel_high = band.astype(jnp.bfloat16)
    kernel_low = (band - kernel_high.astype(jnp.float32)).astype(jnp.bfloat16)
    return (kernel_high, kernel_low)


def convolve(blocks, shifts, weights, span_out):
    span_in = blocks.shape[-1]
    kernel_high, kernel_low = band_kernel(shifts, weights, span_in, span_out)
    flat = blocks.reshape(-1, span_in)
    summed = jnp.dot(flat, kernel_high, preferred_element_type=jnp.float32) + jnp.dot(
        flat, kernel_low, preferred_element_type=jnp.float32
    )
    return summed.astype(jnp.bfloat16).reshape(blocks.shape[:-1] + (span_out,))


def couple_sum(matrices, blocks):
    products = jnp.einsum(
        "kdab,kpbce->kdpace", matrices, blocks, preferred_element_type=jnp.float32
    ).astype(jnp.bfloat16)
    return jnp.einsum("kdpace,kdfc->pafe", products, matrices, preferred_element_type=jnp.float32)


def per_atom(matrices, row_ids, table):

    def one_atom(packed):
        return couple_sum(packed[0], table[packed[1]])

    return lax.map(one_atom, (matrices, row_ids))


def on_device(green, coupling, neighbours, shifts, weights):
    atom_rows = green.shape[0]
    span_out = green.shape[-1]
    device_count = lax.axis_size("atom")
    my_index = lax.axis_index("atom")
    capacity = CAP
    top_rim = from_behind(green[..., :MAXS], "energy", -1)
    extended = jnp.concatenate([green, top_rim], axis=4)
    local_blocks = convolve(extended, shifts, weights, span_out)
    flat_ids = neighbours.reshape(-1)
    owner_of = flat_ids // atom_rows
    local_row = flat_ids % atom_rows
    is_remote = owner_of != my_index
    device_ids = jnp.arange(device_count, dtype=jnp.int32)
    matched = ((owner_of[:, None] == device_ids[None, :]) & is_remote[:, None]).astype(jnp.int32)
    rank_of = jnp.sum(jnp.cumsum(matched, axis=0) * matched, axis=1) - 1
    entry_at = jnp.where(is_remote, owner_of * capacity + rank_of, device_count * capacity)
    request = (
        jnp.zeros((device_count * capacity,), jnp.int32).at[entry_at].set(local_row, mode="drop")
    )
    asked = lax.all_to_all(
        request.reshape(device_count, capacity), "atom", split_axis=0, concat_axis=0, tiled=True
    )
    outgoing = local_blocks[asked.reshape(-1)].reshape(
        (device_count, capacity) + local_blocks.shape[1:]
    )
    incoming = lax.all_to_all(outgoing, "atom", split_axis=0, concat_axis=0, tiled=True)
    incoming = incoming.reshape((device_count * capacity,) + local_blocks.shape[1:])
    matrices = coupling.reshape(atom_rows, NBR, DIRS, ORB, ORB)
    table = jnp.concatenate([local_blocks, incoming], axis=0)
    row_ids = jnp.where(is_remote, atom_rows + entry_at, local_row).reshape(atom_rows, NBR)
    self_energy = per_atom(matrices, row_ids, table)
    return self_energy.astype(jnp.bfloat16)


def solution(mesh):
    placed = (P("atom", None, None, None, "energy"), P("atom", None), P("atom", None), P(), P())
    return jax.shard_map(
        on_device,
        mesh=mesh,
        in_specs=placed,
        out_specs=P("atom", None, None, None, "energy"),
        check_vma=False,
    )
```

profile of v0, /device:TPU:0, one launch (start us, length us, event | category | flops | bytes accessed | tf_op | source)
XLA Modules:
  0.0 87.2 jit_solution(17104053219384284923)
XLA Ops:
  2.0 0.9 %scatter_custom_fusion = s32[16]{0:T(128)S(1)} fusion(s32[96]{0:T(128)S(1)} %fusion.21, s32[96]{0:T(128)S(1)} %and_select_fusion, s32[]{:T(128)} %copy.62), kind=kCustom, calls=%fused_computation.58 | custom fusion | bytes 68 | tf_op jit(solution)/shard_map/scatter | solution.py:74
  3.5 7.3 %all-to-all-start = ((s32[8,1,2]{2,1,0:T(1,128)}), s32[8,1,2]{2,1,0:T(1,128)S(1)}, u32[]{:S(2)}, u32[]{:S(2)}) async-start(s32[8,1,2]{2,1,0:T(1,128)} %bitcast.14), calls=%async_computation | async-start | bytes 8192 | tf_op jit(solution)/shard_map/all_to_all | solution.py:76
  10.8 1.3 %collective-permute-start = (bf16[4,2,12,12,64]{4,1,3,2,0:T(2,128)(2,1)}, bf16[4,2,12,12,64]{4,1,3,2,0:T(2,128)(2,1)S(1)}, u32[]{:S(2)}, u32[]{:S(2)}) collective-permute-start(bf16[4,2,12,12,64]{4,1,3,2,0:T(2,128)(2,1)} %bitcast.64), channel_id=1, source_target_pairs={{8,0},{16,8},{24,16},{9,1},{17,9},{25,17},{10,2},{18,10},{26,18},{... | collective-permute-start | bytes 442376 | tf_op jit(solution)/shard_map/ppermute | solution.py:16
  12.8 0.9 %select_reduce_fusion = f32[192,128]{1,0:T(8,128)S(1)} fusion(f32[16]{0:T(128)} %param.11, s32[16,128]{1,0:T(8,128)S(1)} %iota_add_fusion), kind=kLoop, calls=%fused_computation.22 | loop fusion | flops 1155072 | bytes 106560 | tf_op jit(solution)/shard_map/reduce_sum | solution.py:25
  13.8 3.4 %all-to-all-done = s32[8,1,2]{2,1,0:T(1,128)S(1)} async-done(((s32[8,1,2]{2,1,0:T(1,128)}), s32[8,1,2]{2,1,0:T(1,128)S(1)}, u32[]{:S(2)}, u32[]{:S(2)}) %all-to-all-start) | async-done | bytes 96 | tf_op jit(solution)/shard_map/all_to_all | solution.py:76
  18.5 1.7 %pad_maximum_fusion.1 = bf16[4,2,12,12,192]{4,1,3,2,0:T(2,128)(2,1)S(1)} fusion(bf16[4,2,12,12,64]{4,1,3,2,0:T(2,128)(2,1)S(1)} %collective-permute-done, bf16[4,2,12,12,128]{4,1,3,2,0:T(2,128)(2,1)} %param.7), kind=kLoop, calls=%fused_computation.24 | loop fusion | flops 884736 | bytes 884736 | tf_op jit(solution)/shard_map/concatenate | solution.py:63
  22.2 2.8 %copy.23 = bf16[8,2,2,12,12,128]{5,2,4,3,1,0:T(2,128)(2,1)} copy(bf16[8,2,2,12,12,128]{5,4,3,2,1,0:T(8,128)(2,1)S(1)} %bitcast.62) | data formatting | bytes 2359296 | tf_op jit(solution)/shard_map/reshape | solution.py:79
  25.0 3.7 %all-to-all-start.1 = ((bf16[8,2,2,12,12,128]{5,2,4,3,1,0:T(2,128)(2,1)}), bf16[8,2,2,12,12,128]{5,2,4,3,1,0:T(2,128)(2,1)S(1)}, u32[]{:S(2)}, u32[]{:S(2)}) async-start(bf16[8,2,2,12,12,128]{5,2,4,3,1,0:T(2,128)(2,1)} %copy.23), calls=%async_computation.1 | async-start | bytes 2359296 | tf_op jit(solution)/shard_map/all_to_all | solution.py:82
  28.8 1.2 %reshape.228 = bf16[4,24,3,12,12]{4,3,2,1,0:T(8,128)(2,1)S(1)} reshape(bf16[4,10368]{1,0:T(4,128)(2,1)S(1)} %copy-done) | data formatting | bytes 165888 | tf_op jit(solution)/shard_map/reshape | solution.py:84
  30.1 27.6 %all-to-all-done.1 = bf16[8,2,2,12,12,128]{5,2,4,3,1,0:T(2,128)(2,1)S(1)} async-done(((bf16[8,2,2,12,12,128]{5,2,4,3,1,0:T(2,128)(2,1)}), bf16[8,2,2,12,12,128]{5,2,4,3,1,0:T(2,128)(2,1)S(1)}, u32[]{:S(2)}, u32[]{:S(2)}) %all-to-all-start.1) | async-done | bytes 1179680 | tf_op jit(solution)/shard_map/all_to_all | solution.py:82
  58.1 1.6 %pad_maximum_fusion = bf16[20,2,12,12,128]{4,3,2,1,0:T(8,128)(2,1)} fusion(bf16[16,2,12,12,128]{4,3,2,1,0:T(8,128)(2,1)S(1)} %copy.24, bf16[4,2,12,12,128]{4,3,2,1,0:T(8,128)(2,1)S(1)} %reshape.231), kind=kLoop, calls=%fused_computation.21 | loop fusion | flops 737280 | bytes 2949120 | tf_op jit(solution)/shard_map/concatenate | solution.py:85
  59.7 27.5 %while.10 = (s32[]{:T(128)}, bf16[4,2,12,12,128]{4,1,3,2,0:T(2,128)(2,1)}, bf16[4,24,3,12,12]{4,3,2,1,0:T(8,128)(2,1)S(1)}, s32[4,24]{1,0:T(4,128)S(1)}, bf16[20,2,12,12,128]{4,3,2,1,0:T(8,128)(2,1)}, /*index=5*/s32[]{:T(128)}) while((s32[]{:T(128)}, bf16[4,2,12,12,128]{4,1,3,2,0:T(2,128)(2,1)}, bf16[4,24,3,12,12]{4,3,2,1,0:T(8,128)(2,1)S(1)}, ...), condition=%wide.region_5.6_spmd, body=%wide.region_4.5_spmd.sunk | while | flops 130057288 | bytes 19100624 | solution.py:53
  59.7 2.5 %gather_fusion = bf16[24,2,12,12,128]{4,3,2,1,0:T(8,128)(2,1)S(1)} fusion(bf16[20,2,12,12,128]{4,3,2,1,0:T(8,128)(2,1)} %get-tuple-element.97, s32[1024]{0:T(1024)S(1)} %pad_clamp_fusion.3), kind=kCustom, calls=%fused_computation.clone.1 | custom fusion | bytes 3539040 | tf_op jit(solution)/shard_map/while/body/eval_jaxpr/gather | solution.py:51
  62.2 2.0 %convert_bitcast_fusion.2 = bf16[24,3,2,12,12,128]{5,3,1,4,2,0:T(8,128)(2,1)S(1)} fusion(bf16[24,2,12,12,128,1]{4,3,2,1,0,5:T(8,128)(2,1)S(1)} %bitcast.61, bf16[4,24,3,12,12]{4,3,2,1,0:T(8,128)(2,1)S(1)} %get-tuple-element.95, s32[]{:T(128)} %get-tuple-element.87), kind=kOutput, calls=%fused_computation.5.clone.1 | convolution fusion | flops 66355200 | bytes 7962628 | tf_op jit(solution)/shard_map/while/body/eval_jaxpr/kdab,kpbce->kdpace/dot_general | solution.py:42
  64.2 1.6 %fusion.37 = bf16[1,2,12,12,128]{4,3,2,1,0:T(8,128)(2,1)S(1)} fusion(bf16[24,3,2,12,12,128]{5,3,1,4,2,0:T(8,128)(2,1)S(1)} %convert_bitcast_fusion.2, bf16[4,24,3,12,12]{4,3,2,1,0:T(8,128)(2,1)S(1)} %get-tuple-element.95, s32[]{:T(128)} %get-tuple-element.87), kind=kOutput, calls=%fused_computation.7.clone.1 | convolution fusion | flops 63700992 | bytes 7446532 | tf_op jit(solution)/shard_map/while/body/eval_jaxpr/kdpace,kdfc->pafe/dot_general | solution.py:45
  66.6 2.5 %gather_fusion = bf16[24,2,12,12,128]{4,3,2,1,0:T(8,128)(2,1)S(1)} fusion(bf16[20,2,12,12,128]{4,3,2,1,0:T(8,128)(2,1)} %get-tuple-element.97, s32[1024]{0:T(1024)S(1)} %pad_clamp_fusion.3), kind=kCustom, calls=%fused_computation.clone.1 | custom fusion | bytes 3539040 | tf_op jit(solution)/shard_map/while/body/eval_jaxpr/gather | solution.py:51
  69.1 2.0 %convert_bitcast_fusion.2 = bf16[24,3,2,12,12,128]{5,3,1,4,2,0:T(8,128)(2,1)S(1)} fusion(bf16[24,2,12,12,128,1]{4,3,2,1,0,5:T(8,128)(2,1)S(1)} %bitcast.61, bf16[4,24,3,12,12]{4,3,2,1,0:T(8,128)(2,1)S(1)} %get-tuple-element.95, s32[]{:T(128)} %get-tuple-element.87), kind=kOutput, calls=%fused_computation.5.clone.1 | convolution fusion | flops 66355200 | bytes 7962628 | tf_op jit(solution)/shard_map/while/body/eval_jaxpr/kdab,kpbce->kdpace/dot_general | solution.py:42
  71.1 1.6 %fusion.37 = bf16[1,2,12,12,128]{4,3,2,1,0:T(8,128)(2,1)S(1)} fusion(bf16[24,3,2,12,12,128]{5,3,1,4,2,0:T(8,128)(2,1)S(1)} %convert_bitcast_fusion.2, bf16[4,24,3,12,12]{4,3,2,1,0:T(8,128)(2,1)S(1)} %get-tuple-element.95, s32[]{:T(128)} %get-tuple-element.87), kind=kOutput, calls=%fused_computation.7.clone.1 | convolution fusion | flops 63700992 | bytes 7446532 | tf_op jit(solution)/shard_map/while/body/eval_jaxpr/kdpace,kdfc->pafe/dot_general | solution.py:45
  73.4 2.5 %gather_fusion = bf16[24,2,12,12,128]{4,3,2,1,0:T(8,128)(2,1)S(1)} fusion(bf16[20,2,12,12,128]{4,3,2,1,0:T(8,128)(2,1)} %get-tuple-element.97, s32[1024]{0:T(1024)S(1)} %pad_clamp_fusion.3), kind=kCustom, calls=%fused_computation.clone.1 | custom fusion | bytes 3539040 | tf_op jit(solution)/shard_map/while/body/eval_jaxpr/gather | solution.py:51
  76.0 2.0 %convert_bitcast_fusion.2 = bf16[24,3,2,12,12,128]{5,3,1,4,2,0:T(8,128)(2,1)S(1)} fusion(bf16[24,2,12,12,128,1]{4,3,2,1,0,5:T(8,128)(2,1)S(1)} %bitcast.61, bf16[4,24,3,12,12]{4,3,2,1,0:T(8,128)(2,1)S(1)} %get-tuple-element.95, s32[]{:T(128)} %get-tuple-element.87), kind=kOutput, calls=%fused_computation.5.clone.1 | convolution fusion | flops 66355200 | bytes 7962628 | tf_op jit(solution)/shard_map/while/body/eval_jaxpr/kdab,kpbce->kdpace/dot_general | solution.py:42
  78.0 1.6 %fusion.37 = bf16[1,2,12,12,128]{4,3,2,1,0:T(8,128)(2,1)S(1)} fusion(bf16[24,3,2,12,12,128]{5,3,1,4,2,0:T(8,128)(2,1)S(1)} %convert_bitcast_fusion.2, bf16[4,24,3,12,12]{4,3,2,1,0:T(8,128)(2,1)S(1)} %get-tuple-element.95, s32[]{:T(128)} %get-tuple-element.87), kind=kOutput, calls=%fused_computation.7.clone.1 | convolution fusion | flops 63700992 | bytes 7446532 | tf_op jit(solution)/shard_map/while/body/eval_jaxpr/kdpace,kdfc->pafe/dot_general | solution.py:45
  80.3 2.5 %gather_fusion = bf16[24,2,12,12,128]{4,3,2,1,0:T(8,128)(2,1)S(1)} fusion(bf16[20,2,12,12,128]{4,3,2,1,0:T(8,128)(2,1)} %get-tuple-element.97, s32[1024]{0:T(1024)S(1)} %pad_clamp_fusion.3), kind=kCustom, calls=%fused_computation.clone.1 | custom fusion | bytes 3539040 | tf_op jit(solution)/shard_map/while/body/eval_jaxpr/gather | solution.py:51
  82.9 2.0 %convert_bitcast_fusion.2 = bf16[24,3,2,12,12,128]{5,3,1,4,2,0:T(8,128)(2,1)S(1)} fusion(bf16[24,2,12,12,128,1]{4,3,2,1,0,5:T(8,128)(2,1)S(1)} %bitcast.61, bf16[4,24,3,12,12]{4,3,2,1,0:T(8,128)(2,1)S(1)} %get-tuple-element.95, s32[]{:T(128)} %get-tuple-element.87), kind=kOutput, calls=%fused_computation.5.clone.1 | convolution fusion | flops 66355200 | bytes 7962628 | tf_op jit(solution)/shard_map/while/body/eval_jaxpr/kdab,kpbce->kdpace/dot_general | solution.py:42
  84.9 1.6 %fusion.37 = bf16[1,2,12,12,128]{4,3,2,1,0:T(8,128)(2,1)S(1)} fusion(bf16[24,3,2,12,12,128]{5,3,1,4,2,0:T(8,128)(2,1)S(1)} %convert_bitcast_fusion.2, bf16[4,24,3,12,12]{4,3,2,1,0:T(8,128)(2,1)S(1)} %get-tuple-element.95, s32[]{:T(128)} %get-tuple-element.87), kind=kOutput, calls=%fused_computation.7.clone.1 | convolution fusion | flops 63700992 | bytes 7446532 | tf_op jit(solution)/shard_map/while/body/eval_jaxpr/kdpace,kdfc->pafe/dot_general | solution.py:45
  (43 shorter events, 10.0 us)
Async XLA Ops:
  3.5 13.7 %all-to-all-start = ((s32[8,1,2]{2,1,0:T(1,128)}), s32[8,1,2]{2,1,0:T(1,128)S(1)}, u32[]{:S(2)}, u32[]{:S(2)}) async-start(s32[8,1,2]{2,1,0:T(1,128)} %bitcast.14), calls=%async_computation | async-start | bytes 8192 | tf_op jit(solution)/shard_map/all_to_all | solution.py:76
  10.8 7.7 %collective-permute-start = (bf16[4,2,12,12,64]{4,1,3,2,0:T(2,128)(2,1)}, bf16[4,2,12,12,64]{4,1,3,2,0:T(2,128)(2,1)S(1)}, u32[]{:S(2)}, u32[]{:S(2)}) collective-permute-start(bf16[4,2,12,12,64]{4,1,3,2,0:T(2,128)(2,1)} %bitcast.64), channel_id=1, source_target_pairs={{8,0},{16,8},{24,16},{9,1},{17,9},{25,17},{10,2},{18,10},{26,18},{... | collective-permute-start | bytes 442376 | tf_op jit(solution)/shard_map/ppermute | solution.py:16
  25.0 3.8 %copy-start = (bf16[4,10368]{1,0:T(4,128)(2,1)S(1)}, bf16[4,10368]{1,0:T(4,128)(2,1)}, u32[]{:S(2)}) copy-start(bf16[4,10368]{1,0:T(4,128)(2,1)} %param.8) | copy-start | bytes 248836
  25.0 5.0 %copy-start.1 = (s32[4,24]{1,0:T(4,128)S(1)}, s32[4,24]{1,0:T(4,128)}, u32[]{:S(2)}) copy-start(s32[4,24]{1,0:T(4,128)} %param.9) | copy-start | bytes 1156
  25.0 32.7 %all-to-all-start.1 = ((bf16[8,2,2,12,12,128]{5,2,4,3,1,0:T(2,128)(2,1)}), bf16[8,2,2,12,12,128]{5,2,4,3,1,0:T(2,128)(2,1)S(1)}, u32[]{:S(2)}, u32[]{:S(2)}) async-start(bf16[8,2,2,12,12,128]{5,2,4,3,1,0:T(2,128)(2,1)} %copy.23), calls=%async_computation.1 | async-start | bytes 2359296 | tf_op jit(solution)/shard_map/all_to_all | solution.py:82
where the time goes:
time: 88.5 us; the launch traced here: 87.2 us
  waiting for transfers between devices  31.1 us (35%)
  local copies, waits for them, and re-layouts  22.5 us (25%)
  matrix products  15 us (17%)
  starting transfers between devices  12.3 us (14%)
  other arithmetic  6.14 us (7%)
    all_to_all x1, waiting for transfers between devices, on_device(): lax.all_to_all(outgoing, 'atom', split_axis=0, concat_axis=0, tiled=True)  27.6 us
    gather x4, local copies, waits for them, and re-layouts, one_atom(): return couple_sum(packed[0], table[packed[1]])  10.2 us
    dot_general x4, matrix products, couple_sum(): jnp.einsum('kdab,kpbce->kdpace', matrices, blocks, preferred_element_type...  7.88 us
    all_to_all x1, starting transfers between devices, on_device(): lax.all_to_all(request.reshape(device_count, capacity), 'atom', split_axi...  7.28 us
    dot_general x4, matrix products, couple_sum(): jnp.einsum('kdpace,kdfc->pafe', products, matrices, preferred_element_typ...  6.46 us
    all_to_all x1, starting transfers between devices, on_device(): lax.all_to_all(outgoing, 'atom', split_axis=0, concat_axis=0, tiled=True)  3.69 us
    all_to_all x1, waiting for transfers between devices, on_device(): lax.all_to_all(request.reshape(device_count, capacity), 'atom', split_axi...  3.42 us
    dynamic_update_slice x4, local copies, waits for them, and re-layouts, per_atom(): return lax.map(one_atom, (matrices, row_ids))  2.88 us
  transfers between devices with their start and end apart: 3, of which 2 were waited for; matrix products, arithmetic and copies ran while one was open for 5% of the time, Pallas kernels for 0%

commit v1 on v0

v1 whole, which is shorter than its diff:
```python
import jax
import jax.numpy as jnp
from jax import lax
from jax.experimental import pallas as pl
from jax.experimental.pallas import tpu as pltpu
from jax.sharding import PartitionSpec as P

MAXS = 64
CAP = 2
LANES = 128
PAD = 16
BF, F32, I32 = jnp.bfloat16, jnp.float32, jnp.int32
VM = pl.BlockSpec(memory_space=pltpu.VMEM)
SM = pl.BlockSpec(memory_space=pltpu.SMEM)
LIMIT = 40 * 2**20


def call(body, outs, ins, out_specs=None, scratch=(), flops=0, moved=0):
    return pl.pallas_call(
        body,
        out_shape=outs,
        in_specs=ins,
        out_specs=out_specs or [VM] * len(outs),
        scratch_shapes=list(scratch),
        compiler_params=pltpu.CompilerParams(vmem_limit_bytes=LIMIT),
        cost_estimate=pl.CostEstimate(flops=flops, bytes_accessed=moved, transcendentals=0),
    )


def dot(x, y):
    return jnp.dot(x, y, preferred_element_type=F32)


def iota(shape, dim):
    return lax.broadcasted_iota(I32, shape, dim)


def owner_row(entry, rows):
    if rows & (rows - 1) == 0:
        return lax.shift_right_logical(entry, rows.bit_length() - 1), lax.bitwise_and(entry, rows - 1)
    return lax.div(entry, rows), lax.rem(entry, rows)


def bands(shifts, weights, span):
    half = span // 2
    shape = (2 * span, span)
    lane = iota(shape, 1)
    gap = iota(shape, 0) - half - jnp.where(lane < half, lane, lane - half)
    band = jnp.zeros(shape, F32)
    for q in range(shifts.shape[0]):
        band = band + jnp.where(gap == shifts[q], weights[q], 0.0)
    high = band.astype(BF).astype(F32)
    return band, high, lane < half


def parted(part, first):
    zero = jnp.zeros_like(part)
    return jnp.concatenate([jnp.where(first, part, zero), jnp.where(first, zero, part)], axis=0).astype(BF)


def rows_apart(x, atoms):
    block = x.shape[0] // atoms
    size = block // 2
    to, of = iota((block, block), 0), iota((block, block), 1)
    pick = (of == jnp.where(to < size, 2 * to, 2 * (to - size) + 1)).astype(F32).astype(BF)
    wide = jnp.concatenate([x[a * block : (a + 1) * block] for a in range(atoms)], axis=1)
    return dot(pick, wide).astype(BF)


def beside(parts, atoms, span, size):
    stacked = []
    for a in range(atoms):
        stacked.append(
            jnp.concatenate(
                [y[p * size : (p + 1) * size, a * span : (a + 1) * span] for p in range(2) for y in parts], axis=1
            )
        )
    return jnp.concatenate(stacked, axis=0)


def low_kernel(shifts, weights, x, out):
    atoms, size, span = out.shape
    band, high, first = bands(shifts, weights, span)
    half = span // 2
    z = beside([rows_apart(x[...], atoms)], atoms, span, size)
    cut, first = slice(half, half + span), first[half : half + span]
    y = dot(z, parted(high[cut], first)) + dot(z, parted((band - high)[cut], first))
    out[...] = y.astype(BF).reshape(out.shape)


def high_kernel(shifts, weights, x, beyond, out):
    atoms, size, span = out.shape
    band, high, first = bands(shifts, weights, span)
    z = beside([rows_apart(x[...], atoms), rows_apart(beyond[...], atoms)], atoms, span, size)
    y = dot(z, parted(high, first)) + dot(z, parted(band - high, first))
    out[...] = y.astype(BF).reshape(out.shape)


def asked_by(names, holder, rows):
    def step(k, found):
        for a in range(names.shape[0]):
            owner, row = owner_row(names[a, k], rows)
            out = []
            for (count, picks), who in zip(found, holder):
                hit = owner == who
                picks = tuple(jnp.where(hit & (count == r), row, p) for r, p in enumerate(picks))
                out.append((count + hit.astype(I32), picks))
            found = tuple(out)
        return found

    zero = jnp.int32(0)
    start = tuple((zero, (zero,) * CAP) for _ in holder)
    return [picks for _, picks in lax.fori_loop(0, names.shape[1], step, start)]


def make_own(mates, half):
    def kernel(*refs):
        names, (low, high), outs, later = refs[:mates], refs[mates : mates + 2], refs[mates + 2 : -1], refs[-1]
        rows, _, span = low.shape
        me = lax.axis_index("atom")
        for s in range(mates):
            own, mirrored = asked_by(names[s], (me, lax.bitwise_xor(me, half)), rows)
            for r in range(CAP):
                outs[s][r, :, :span] = low[own[r]]
                outs[s][r, :, span:] = high[own[r]]
                later[s * CAP + r] = mirrored[r]

    return kernel


def make_relay(mates):
    def kernel(*refs):
        later, (low, high), outs = refs[0], refs[1:3], refs[3:]
        span = low.shape[2]
        for s in range(mates):
            for r in range(CAP):
                outs[s][r, :, :span] = low[later[s * CAP + r]]
                outs[s][r, :, span:] = high[later[s * CAP + r]]

    return kernel


def make_form(orb):
    size = orb * orb

    def kernel(names, x, ops_local, ops_far, place, left, right, local, count):
        atoms, nbr = names.shape
        terms = x.shape[0]
        dirs = terms // (atoms * nbr)
        me = lax.axis_index("atom")
        chunks = left.shape[0]
        wide = chunks * LANES
        source, lane = iota((size, wide), 0), iota((size, wide), 1)
        group = sum(((lane >= m * orb).astype(I32) for m in range(1, orb)), jnp.zeros((size, wide), I32))
        within = lane - group * orb
        real = lane < size
        values = x[...]
        zeros = jnp.zeros((terms, wide), F32)
        for i in range(PAD):
            if i < orb:
                spread = dot(values, ((source == i * orb + group) & real).astype(F32).astype(BF))
                filled = dot(values, ((source == i * orb + within) & real).astype(F32).astype(BF))
                for c in range(chunks):
                    left[c, i] = spread[:, c * LANES : (c + 1) * LANES]
            else:
                filled = zeros
            for c in range(chunks):
                right[c, pl.ds(i, terms, stride=PAD), :] = filled[:, c * LANES : (c + 1) * LANES]
        local[...] = jnp.zeros(local.shape, F32)
        for w in range(count.shape[0]):
            count[w] = 0
        for q in range(place.shape[0]):
            place[q] = -1

        def operator(base):
            for c in range(chunks):
                lanes = slice(c * LANES, (c + 1) * LANES)
                tiles = [right[c, pl.ds(pl.multiple_of((base + d) * PAD, PAD), PAD), :] for d in range(dirs)]
                for i in range(orb):
                    rows = [left[c, i, pl.ds(base + d, 1), :] * tiles[d] for d in range(dirs)]
                    yield slice(i * PAD, (i + 1) * PAD), lanes, sum(rows[1:], rows[0])

        def entry(k, carry):
            for a in range(atoms):
                base = (a * nbr + k) * dirs
                owner, row = owner_row(names[a, k], atoms)
                apart = lax.bitwise_xor(owner, me)

                @pl.when(apart == 0)
                def _():
                    for at, lanes, tile in operator(base):
                        local[a * atoms + row, at, lanes] += tile

                @pl.when(apart != 0)
                def _():
                    rank = count[owner]
                    count[owner] = rank + 1
                    slot = (apart - 1) * CAP + jnp.minimum(rank, CAP - 1)
                    place[slot] = a * atoms + row
                    for at, lanes, tile in operator(base):
                        ops_far[slot, at, lanes] = tile.astype(BF)

            return carry

        lax.fori_loop(0, nbr, entry, 0)
        ops_local[...] = local[...].astype(BF)

    return kernel


def make_final(mates, orb):
    size = orb * orb

    def kernel(*refs):
        place, ops_local, ops_far = refs[:3]
        own, mirror = refs[3:5], refs[5:7]
        near, far = refs[7 : 7 + mates], refs[7 + mates : 7 + 2 * mates]
        out, total = refs[-2:]
        atoms, tall, wide = total.shape
        span = wide // 2
        half = span // 2
        for a in range(atoms):
            run = jnp.zeros((tall, wide), F32)
            for b in range(atoms):
                run = run + dot(ops_local[a * atoms + b, :, :size], jnp.concatenate([own[0][b], own[1][b]], axis=1))
            total[a] = run

        def add(slot, block):
            spot = place[slot]

            @pl.when(spot >= 0)
            def _():
                to, row = owner_row(spot, atoms)
                total[to] += dot(ops_far[slot, :, :size], block(row))

        for s in range(mates):
            for r in range(CAP):
                add(s * CAP + r, lambda row: near[s][r])
        for r in range(CAP):
            add(mates * CAP + r, lambda row: jnp.concatenate([mirror[0][row], mirror[1][row]], axis=1))
        for s in range(mates):
            for r in range(CAP):
                add((mates + 1 + s) * CAP + r, lambda row: far[s][r])

        to, of = iota((2 * size, tall), 0), iota((2 * size, tall), 1)
        f = lax.bitwise_and(of, PAD - 1)
        at = 2 * (lax.shift_right_logical(of, PAD.bit_length() - 1) * orb + f)
        even = ((to == at) & (f < orb)).astype(F32).astype(BF)
        odd = ((to == at + 1) & (f < orb)).astype(F32).astype(BF)
        parts = [[], []]
        for a in range(atoms):
            for p in range(2):
                lanes = [total[a, :, h * span + p * half : h * span + (p + 1) * half] for h in range(2)]
                parts[p].append(jnp.concatenate(lanes, axis=1).astype(BF))
        rows = dot(even, jnp.concatenate(parts[0], axis=1)) + dot(odd, jnp.concatenate(parts[1], axis=1))
        for a in range(atoms):
            out[a * 2 * size : (a + 1) * 2 * size, :] = rows[:, a * span : (a + 1) * span].astype(BF)

    return kernel


def on_device(green, coupling, neighbours, shifts, weights):
    atoms, _, orb, _, span = green.shape
    size = orb * orb
    devices = lax.axis_size("atom")
    half = devices // 2
    mates = half - 1
    peers = lax.axis_size("energy")
    shape = jax.ShapeDtypeStruct

    def across(value, by):
        return lax.ppermute(value, "atom", [(i, i ^ by) for i in range(devices)])

    x = green.transpose(0, 2, 3, 1, 4).reshape(atoms * size * 2, span)
    beyond = lax.ppermute(x, "energy", [(i, i - 1) for i in range(1, peers)])
    unit = shape((atoms, size, span), BF)
    (low,) = call(low_kernel, [unit], [SM, SM, VM])(shifts, weights, x)
    (high,) = call(high_kernel, [unit], [SM, SM, VM, VM])(shifts, weights, x, beyond)
    mirror = across(low, half), across(high, half)
    names = [across(neighbours, s) for s in range(1, half)]

    pair = shape((CAP, size, 2 * span), BF)
    *own_out, later = call(
        make_own(mates, half),
        [pair] * mates + [shape((mates * CAP,), I32)],
        [SM] * mates + [VM] * 2,
        [VM] * mates + [SM],
    )(*names, low, high)
    near = [across(v, s + 1) for s, v in enumerate(own_out)]

    terms = coupling.reshape(-1, size)
    tall, wide = orb * PAD, pl.cdiv(size, LANES) * LANES
    far_slots = (devices - 1) * CAP
    ops_local, ops_far, place = call(
        make_form(orb),
        [shape((atoms * atoms, tall, wide), BF), shape((far_slots, tall, wide), BF), shape((far_slots,), I32)],
        [SM, VM],
        [VM, VM, SM],
        [
            pltpu.VMEM((wide // LANES, orb, terms.shape[0], LANES), F32),
            pltpu.VMEM((wide // LANES, terms.shape[0] * PAD, LANES), F32),
            pltpu.VMEM((atoms * atoms, tall, wide), F32),
            pltpu.SMEM((devices,), I32),
        ],
        flops=4 * 10**9,
        moved=8 * 10**6,
    )(neighbours, terms)

    relay_out = call(make_relay(mates), [pair] * mates, [SM, VM, VM])(later, *mirror)
    far = [across(v, s + 1) for s, v in enumerate(relay_out)]
    (out,) = call(
        make_final(mates, orb),
        [shape(x.shape, BF)],
        [SM] + [VM] * (6 + 2 * mates),
        None,
        [pltpu.VMEM((atoms, tall, 2 * span), F32)],
    )(place, ops_local, ops_far, low, high, *mirror, *near, *far)
    return out.reshape(atoms, orb, orb, 2, span).transpose(0, 3, 1, 2, 4)


def solution(mesh):
    placed = (P("atom", None, None, None, "energy"), P("atom", None), P("atom", None), P(), P())
    return jax.shard_map(
        on_device,
        mesh=mesh,
        in_specs=placed,
        out_specs=P("atom", None, None, None, "energy"),
        check_vma=False,
    )
```

time: 88.5 us -> 44.7 us (0.51); the launches traced: 87.2 us -> 44.5 us
  waiting for transfers between devices: 31.1 us -> 3.85 us
  Pallas kernels: 0 us -> 20.9 us
  local copies, waits for them, and re-layouts: 22.5 us -> 3.4 us
  matrix products: 15 us -> 0 us
  other arithmetic: 6.14 us -> 0 us
  starting transfers between devices: 12.3 us -> 16.2 us
    all_to_all x2 -> x0, waiting for transfers between devices: 31.1 us -> none  [the longest x1 27.6 us: on_device(): lax.all_to_all(outgoing, 'atom', split_axis=0, concat_axis=0, tiled=True)]
    pallas_call x0 -> x6, Pallas kernels: none -> 20.9 us  [the longest x1 9.79 us: on_device(): call(make_form(orb), [shape((atoms * atoms, tall, wide), BF), shape((far_...]
    dot_general x10 -> x0, matrix products: 15 us -> none  [the longest x4 7.88 us: couple_sum(): jnp.einsum('kdab,kpbce->kdpace', matrices, blocks, preferred_element_type...]
    ppermute x1 -> x12, starting transfers between devices: 1.28 us -> 16.2 us  [the longest x11 14.9 us: across(): return lax.ppermute(value, 'atom', [(i, i ^ by) for i in range(devices)])]
    gather x5 -> x0, local copies, waits for them, and re-layouts: 11 us -> none  [the longest x4 10.2 us: one_atom(): return couple_sum(packed[0], table[packed[1]])]
    all_to_all x2 -> x0, starting transfers between devices: 11 us -> none  [the longest x1 7.28 us: on_device(): lax.all_to_all(request.reshape(device_count, capacity), 'atom', split_axi...]
    reshape x8 -> x1, local copies, waits for them, and re-layouts: 6.37 us -> 1.12 us  [on_device(): terms = coupling.reshape(-1, size)]
    ppermute x1 -> x12, waiting for transfers between devices: 0.01 us -> 3.85 us  [the longest x11 3.85 us: across(): return lax.ppermute(value, 'atom', [(i, i ^ by) for i in range(devices)])]
  transfers between devices with their start and end apart: 3 -> 12, of which waited for: 2 -> 2; matrix products, arithmetic and copies ran while one was open for 5% -> 3% of each run, Pallas kernels for 0% -> 38%
where the time goes in v1:
time: 44.7 us; the launch traced here: 44.5 us
  Pallas kernels  20.9 us (47%)
  starting transfers between devices  16.2 us (36%)
  waiting for transfers between devices  3.85 us (9%)
  local copies, waits for them, and re-layouts  3.4 us (8%)
    ppermute x11, starting transfers between devices, across(): return lax.ppermute(value, 'atom', [(i, i ^ by) for i in range(devices)])  14.9 us
    pallas_call x1, Pallas kernels, on_device(): call(make_form(orb), [shape((atoms * atoms, tall, wide), BF), shape((far_...  9.79 us
    pallas_call x1, Pallas kernels, on_device(): call(make_final(mates, orb), [shape(x.shape, BF)], [SM] + [VM] * (6 + 2 *...  4.22 us
    ppermute x11, waiting for transfers between devices, across(): return lax.ppermute(value, 'atom', [(i, i ^ by) for i in range(devices)])  3.85 us
    pallas_call x1, Pallas kernels, on_device(): call(make_own(mates, half), [pair] * mates + [shape((mates * CAP,), I32)]...  3.71 us
    unnamed x8, local copies, waits for them, and re-layouts  2.27 us
    pallas_call x1, Pallas kernels, on_device(): call(high_kernel, [unit], [SM, SM, VM, VM])(shifts, weights, x, beyond)  1.47 us
    ppermute x1, starting transfers between devices, on_device(): beyond = lax.ppermute(x, 'energy', [(i, i - 1) for i in range(1, peers)])  1.28 us
  transfers between devices with their start and end apart: 12, of which 2 were waited for; matrix products, arithmetic and copies ran while one was open for 3% of the time, Pallas kernels for 38%

profile of v1, /device:TPU:0, one launch (start us, length us, event | category | flops | bytes accessed | tf_op | source)
XLA Modules:
  0.0 44.5 jit_solution(4954928649733752718)
XLA Ops:
  0.0 1.3 %collective-permute-start = (bf16[1152,128]{1,0:T(8,128)(2,1)}, bf16[1152,128]{1,0:T(8,128)(2,1)S(1)}, u32[]{:S(2)}, u32[]{:S(2)}) collective-permute-start(bf16[1152,128]{1,0:T(8,128)(2,1)} %bitcast.6), channel_id=1, source_target_pairs={{8,0},{16,8},{24,16},{9,1},{17,9},{25,17},{10,2},{18,10},{26,18},{... | collective-permute-start | bytes 884744 | tf_op jit(solution)/shard_map/ppermute | solution.py:275
  1.3 3.0 %collective-permute-start.3 = (s32[4,24]{1,0:T(4,128)}, s32[4,24]{1,0:T(4,128)S(1)}, u32[]{:S(2)}, u32[]{:S(2)}) collective-permute-start(s32[4,24]{1,0:T(4,128)} %names.1), channel_id=1, source_target_pairs={{0,1},{1,0},{2,3},{3,2},{4,5},{5,4},{6,7},{7,6},{8,9},{9,8},{10,11... | collective-permute-start | bytes 1160 | tf_op jit(solution)/shard_map/ppermute | solution.py:272
  4.3 1.5 %collective-permute-start.5 = (s32[4,24]{1,0:T(4,128)}, s32[4,24]{1,0:T(4,128)S(1)}, u32[]{:S(2)}, u32[]{:S(2)}) collective-permute-start(s32[4,24]{1,0:T(4,128)} %names.1), channel_id=1, source_target_pairs={{0,3},{1,2},{2,1},{3,0},{4,7},{5,6},{6,5},{7,4},{8,11},{9,10},{10,... | collective-permute-start | bytes 1160 | tf_op jit(solution)/shard_map/ppermute | solution.py:272
  5.8 0.1 collective-permute-start.4
  5.9 1.0 %copy-done = bf16[4,2,12,12,128]{4,1,3,2,0:T(2,128)(2,1)S(1)} copy-done((bf16[4,2,12,12,128]{4,1,3,2,0:T(2,128)(2,1)S(1)}, bf16[4,2,12,12,128]{4,1,3,2,0:T(2,128)(2,1)}, u32[]{:S(2)}) %copy-start) | copy-done | bytes 294936
  6.9 0.7 %copy-done.1 = s32[16]{0:T(128)S(1)} copy-done((s32[16]{0:T(128)S(1)}, s32[16]{0:T(128)}, u32[]{:S(2)}) %copy-start.1) | copy-done | bytes 88
  7.5 0.7 %copy-done.2 = f32[16]{0:T(128)S(1)} copy-done((f32[16]{0:T(128)S(1)}, f32[16]{0:T(128)}, u32[]{:S(2)}) %copy-start.2) | copy-done | bytes 88
  8.2 1.1 %shard_map.56.refs_3_ = bf16[4,144,128]{2,1,0:T(8,128)(2,1)S(1)} custom-call(s32[16]{0:T(128)S(1)} %copy-done.1, f32[16]{0:T(128)S(1)} %copy-done.2, bf16[1152,128]{1,0:T(8,128)(2,1)S(1)} %bitcast.7), custom_call_target="tpu_custom_call" | custom-call | tf_op jit(solution)/shard_map/pallas_call | solution.py:277
  9.3 3.0 %collective-permute-start.1 = (bf16[4,144,128]{2,1,0:T(8,128)(2,1)S(1)}, bf16[4,144,128]{2,1,0:T(8,128)(2,1)S(1)}, u32[]{:S(2)}, u32[]{:S(2)}) collective-permute-start(bf16[4,144,128]{2,1,0:T(8,128)(2,1)S(1)} %shard_map.56.refs_3_), channel_id=1, source_target_pairs={{0,4},{1,5},{2,6},{3,7},{4,0},{5,1},{6,2},{7,3},{8,12},{9,13},{10,... | collective-permute-start | bytes 442376 | tf_op jit(solution)/shard_map/ppermute | solution.py:272
  12.3 1.5 %shard_map.57.refs_4_ = bf16[4,144,128]{2,1,0:T(8,128)(2,1)S(1)} custom-call(s32[16]{0:T(128)S(1)} %copy-done.1, f32[16]{0:T(128)S(1)} %copy-done.2, bf16[1152,128]{1,0:T(8,128)(2,1)S(1)} %bitcast.8, bf16[1152,128]{1,0:T(8,128)(2,1)S(1)} %collective-permute-done.beyond), custom_call_target="tpu_custom_call" | custom-call | tf_op jit(solution)/shard_map/pallas_call | solution.py:278
  13.8 0.1 collective-permute-start.2
  13.9 3.7 %shard_map.58 = (bf16[2,144,256]{2,1,0:T(8,128)(2,1)S(1)}, bf16[2,144,256]{2,1,0:T(8,128)(2,1)S(1)}, bf16[2,144,256]{2,1,0:T(8,128)(2,1)S(1)}, s32[6]{0:T(128)S(1)}) custom-call(s32[4,24]{1,0:T(4,128)S(1)} %collective-permute-done.3.refs_0_, s32[4,24]{1,0:T(4,128)S(1)} %collective-permute-done.4.refs_1_, s32[4,24]{1,0:T(4,128)S(1)} %collective-permute-done.5.refs_2_, ...), custom_call_target="tpu_custom_call" | custom-call | tf_op jit(solution)/shard_map/pallas_call | solution.py:283
  17.6 1.9 %collective-permute-start.6 = (bf16[2,144,256]{2,1,0:T(8,128)(2,1)S(1)}, bf16[2,144,256]{2,1,0:T(8,128)(2,1)S(1)}, u32[]{:S(2)}, u32[]{:S(2)}) collective-permute-start(bf16[2,144,256]{2,1,0:T(8,128)(2,1)S(1)} %get-tuple-element.18), channel_id=1, source_target_pairs={{0,1},{1,0},{2,3},{3,2},{4,5},{5,4},{6,7},{7,6},{8,9},{9,8},{10,11... | collective-permute-start | bytes 442376 | tf_op jit(solution)/shard_map/ppermute | solution.py:272
  19.5 1.1 %reshape.9.x = bf16[288,144]{1,0:T(8,128)(2,1)S(1)} reshape(bf16[4,10368]{1,0:T(4,128)(2,1)} %param.6) | data formatting | bytes 165888 | tf_op jit(solution)/shard_map/reshape | solution.py:291
  20.7 1.6 %collective-permute-start.7 = (bf16[2,144,256]{2,1,0:T(8,128)(2,1)S(1)}, bf16[2,144,256]{2,1,0:T(8,128)(2,1)S(1)}, u32[]{:S(2)}, u32[]{:S(2)}) collective-permute-start(bf16[2,144,256]{2,1,0:T(8,128)(2,1)S(1)} %get-tuple-element.19), channel_id=1, source_target_pairs={{0,2},{1,3},{2,0},{3,1},{4,6},{5,7},{6,4},{7,5},{8,10},{9,11},{10,... | collective-permute-start | bytes 442376 | tf_op jit(solution)/shard_map/ppermute | solution.py:272
  22.3 0.1 collective-permute-start.8
  22.4 0.9 %collective-permute-done.1.refs_1_.refs_5_ = bf16[4,144,128]{2,1,0:T(8,128)(2,1)S(1)} collective-permute-done((bf16[4,144,128]{2,1,0:T(8,128)(2,1)S(1)}, bf16[4,144,128]{2,1,0:T(8,128)(2,1)S(1)}, u32[]{:S(2)}, u32[]{:S(2)}) %collective-permute-start.1) | collective-permute-done | bytes 147488 | tf_op jit(solution)/shard_map/ppermute | solution.py:272
  23.3 2.9 %collective-permute-done.2.refs_2_.refs_6_ = bf16[4,144,128]{2,1,0:T(8,128)(2,1)S(1)} collective-permute-done((bf16[4,144,128]{2,1,0:T(8,128)(2,1)S(1)}, bf16[4,144,128]{2,1,0:T(8,128)(2,1)S(1)}, u32[]{:S(2)}, u32[]{:S(2)}) %collective-permute-start.2) | collective-permute-done | bytes 147488 | tf_op jit(solution)/shard_map/ppermute | solution.py:272
  26.2 0.6 %shard_map.59 = (bf16[2,144,256]{2,1,0:T(8,128)(2,1)S(1)}, bf16[2,144,256]{2,1,0:T(8,128)(2,1)S(1)}, bf16[2,144,256]{2,1,0:T(8,128)(2,1)S(1)}) custom-call(s32[6]{0:T(128)S(1)} %get-tuple-element.21.refs_0_, bf16[4,144,128]{2,1,0:T(8,128)(2,1)S(1)} %collective-permute-done.1.refs_1_.refs_5_, bf16[4,144,128]{2,1,0:T(8,128)(2,1)S(1)} %collective-permute-done.2.refs_2_.refs_6_), custom_call_target="tpu_custom_call" | custom-call | tf_op jit(solution)/shard_map/pallas_call | solution.py:309
  26.8 1.6 %collective-permute-start.9 = (bf16[2,144,256]{2,1,0:T(8,128)(2,1)S(1)}, bf16[2,144,256]{2,1,0:T(8,128)(2,1)S(1)}, u32[]{:S(2)}, u32[]{:S(2)}) collective-permute-start(bf16[2,144,256]{2,1,0:T(8,128)(2,1)S(1)} %get-tuple-element.22), channel_id=1, source_target_pairs={{0,1},{1,0},{2,3},{3,2},{4,5},{5,4},{6,7},{7,6},{8,9},{9,8},{10,11... | collective-permute-start | bytes 442376 | tf_op jit(solution)/shard_map/ppermute | solution.py:272
  28.5 0.6 %collective-permute-start.10 = (bf16[2,144,256]{2,1,0:T(8,128)(2,1)S(1)}, bf16[2,144,256]{2,1,0:T(8,128)(2,1)S(1)}, u32[]{:S(2)}, u32[]{:S(2)}) collective-permute-start(bf16[2,144,256]{2,1,0:T(8,128)(2,1)S(1)} %get-tuple-element.23), channel_id=1, source_target_pairs={{0,2},{1,3},{2,0},{3,1},{4,6},{5,7},{6,4},{7,5},{8,10},{9,11},{10,... | collective-permute-start | bytes 442376 | tf_op jit(solution)/shard_map/ppermute | solution.py:272
  29.1 1.3 %collective-permute-start.11 = (bf16[2,144,256]{2,1,0:T(8,128)(2,1)S(1)}, bf16[2,144,256]{2,1,0:T(8,128)(2,1)S(1)}, u32[]{:S(2)}, u32[]{:S(2)}) collective-permute-start(bf16[2,144,256]{2,1,0:T(8,128)(2,1)S(1)} %get-tuple-element.24), channel_id=1, source_target_pairs={{0,3},{1,2},{2,1},{3,0},{4,7},{5,6},{6,5},{7,4},{8,11},{9,10},{10,... | collective-permute-start | bytes 442376 | tf_op jit(solution)/shard_map/ppermute | solution.py:272
  30.4 9.8 %shard_map.55 = (bf16[16,192,256]{2,1,0:T(8,128)(2,1)S(1)}, bf16[14,192,256]{2,1,0:T(8,128)(2,1)S(1)}, s32[14]{0:T(128)S(1)}) custom-call(s32[4,24]{1,0:T(4,128)S(1)} %copy-done.3, bf16[288,144]{1,0:T(8,128)(2,1)S(1)} %reshape.9.x), custom_call_target="tpu_custom_call" | custom-call | flops 4000000000 | bytes 8000000 | tf_op jit(solution)/shard_map/pallas_call | solution.py:294
  40.3 4.2 %shard_map.60 = bf16[1152,128]{1,0:T(8,128)(2,1)} custom-call(s32[14]{0:T(128)S(1)} %get-tuple-element.15.refs_0_, bf16[16,192,256]{2,1,0:T(8,128)(2,1)S(1)} %get-tuple-element.16.refs_1_, bf16[14,192,256]{2,1,0:T(8,128)(2,1)S(1)} %get-tuple-element.17.refs_2_, bf16[4,144,128]{2,1,0:T(8,128)(2,1)S(1)} %shard_map.56.refs_3_, ...), custom_call_target="tpu_custom_call" | custom-call | tf_op jit(solution)/shard_map/pallas_call | solution.py:311
  (15 shorter events, 0.0 us)
Async XLA Ops:
  0.0 12.3 %collective-permute-start = (bf16[1152,128]{1,0:T(8,128)(2,1)}, bf16[1152,128]{1,0:T(8,128)(2,1)S(1)}, u32[]{:S(2)}, u32[]{:S(2)}) collective-permute-start(bf16[1152,128]{1,0:T(8,128)(2,1)} %bitcast.6), channel_id=1, source_target_pairs={{8,0},{16,8},{24,16},{9,1},{17,9},{25,17},{10,2},{18,10},{26,18},{... | collective-permute-start | bytes 884744 | tf_op jit(solution)/shard_map/ppermute | solution.py:275
  1.3 12.6 %collective-permute-start.3 = (s32[4,24]{1,0:T(4,128)}, s32[4,24]{1,0:T(4,128)S(1)}, u32[]{:S(2)}, u32[]{:S(2)}) collective-permute-start(s32[4,24]{1,0:T(4,128)} %names.1), channel_id=1, source_target_pairs={{0,1},{1,0},{2,3},{3,2},{4,5},{5,4},{6,7},{7,6},{8,9},{9,8},{10,11... | collective-permute-start | bytes 1160 | tf_op jit(solution)/shard_map/ppermute | solution.py:272
  4.3 9.6 %collective-permute-start.5 = (s32[4,24]{1,0:T(4,128)}, s32[4,24]{1,0:T(4,128)S(1)}, u32[]{:S(2)}, u32[]{:S(2)}) collective-permute-start(s32[4,24]{1,0:T(4,128)} %names.1), channel_id=1, source_target_pairs={{0,3},{1,2},{2,1},{3,0},{4,7},{5,6},{6,5},{7,4},{8,11},{9,10},{10,... | collective-permute-start | bytes 1160 | tf_op jit(solution)/shard_map/ppermute | solution.py:272
  5.8 8.1 %collective-permute-start.4 = (s32[4,24]{1,0:T(4,128)}, s32[4,24]{1,0:T(4,128)S(1)}, u32[]{:S(2)}, u32[]{:S(2)}) collective-permute-start(s32[4,24]{1,0:T(4,128)} %names.1), channel_id=1, source_target_pairs={{0,2},{1,3},{2,0},{3,1},{4,6},{5,7},{6,4},{7,5},{8,10},{9,11},{10,... | collective-permute-start | bytes 1160 | tf_op jit(solution)/shard_map/ppermute | solution.py:272
  5.9 1.0 %copy-start = (bf16[4,2,12,12,128]{4,1,3,2,0:T(2,128)(2,1)S(1)}, bf16[4,2,12,12,128]{4,1,3,2,0:T(2,128)(2,1)}, u32[]{:S(2)}) copy-start(bf16[4,2,12,12,128]{4,1,3,2,0:T(2,128)(2,1)} %param.5) | copy-start | bytes 884740
  6.9 0.7 %copy-start.1 = (s32[16]{0:T(128)S(1)}, s32[16]{0:T(128)}, u32[]{:S(2)}) copy-start(s32[16]{0:T(128)} %shifts.3) | copy-start | bytes 196
  7.5 0.7 %copy-start.2 = (f32[16]{0:T(128)S(1)}, f32[16]{0:T(128)}, u32[]{:S(2)}) copy-start(f32[16]{0:T(128)} %weights.3) | copy-start | bytes 196
  8.2 22.2 %copy-start.3 = (s32[4,24]{1,0:T(4,128)S(1)}, s32[4,24]{1,0:T(4,128)}, u32[]{:S(2)}) copy-start(s32[4,24]{1,0:T(4,128)} %names.1) | copy-start | bytes 1156
  9.3 14.0 %collective-permute-start.1 = (bf16[4,144,128]{2,1,0:T(8,128)(2,1)S(1)}, bf16[4,144,128]{2,1,0:T(8,128)(2,1)S(1)}, u32[]{:S(2)}, u32[]{:S(2)}) collective-permute-start(bf16[4,144,128]{2,1,0:T(8,128)(2,1)S(1)} %shard_map.56.refs_3_), channel_id=1, source_target_pairs={{0,4},{1,5},{2,6},{3,7},{4,0},{5,1},{6,2},{7,3},{8,12},{9,13},{10,... | collective-permute-start | bytes 442376 | tf_op jit(solution)/shard_map/ppermute | solution.py:272
  13.8 12.4 %collective-permute-start.2 = (bf16[4,144,128]{2,1,0:T(8,128)(2,1)S(1)}, bf16[4,144,128]{2,1,0:T(8,128)(2,1)S(1)}, u32[]{:S(2)}, u32[]{:S(2)}) collective-permute-start(bf16[4,144,128]{2,1,0:T(8,128)(2,1)S(1)} %shard_map.57.refs_4_), channel_id=1, source_target_pairs={{0,4},{1,5},{2,6},{3,7},{4,0},{5,1},{6,2},{7,3},{8,12},{9,13},{10,... | collective-permute-start | bytes 442376 | tf_op jit(solution)/shard_map/ppermute | solution.py:272
  17.6 11.5 %collective-permute-start.6 = (bf16[2,144,256]{2,1,0:T(8,128)(2,1)S(1)}, bf16[2,144,256]{2,1,0:T(8,128)(2,1)S(1)}, u32[]{:S(2)}, u32[]{:S(2)}) collective-permute-start(bf16[2,144,256]{2,1,0:T(8,128)(2,1)S(1)} %get-tuple-element.18), channel_id=1, source_target_pairs={{0,1},{1,0},{2,3},{3,2},{4,5},{5,4},{6,7},{7,6},{8,9},{9,8},{10,11... | collective-permute-start | bytes 442376 | tf_op jit(solution)/shard_map/ppermute | solution.py:272
  20.7 19.5 %collective-permute-start.7 = (bf16[2,144,256]{2,1,0:T(8,128)(2,1)S(1)}, bf16[2,144,256]{2,1,0:T(8,128)(2,1)S(1)}, u32[]{:S(2)}, u32[]{:S(2)}) collective-permute-start(bf16[2,144,256]{2,1,0:T(8,128)(2,1)S(1)} %get-tuple-element.19), channel_id=1, source_target_pairs={{0,2},{1,3},{2,0},{3,1},{4,6},{5,7},{6,4},{7,5},{8,10},{9,11},{10,... | collective-permute-start | bytes 442376 | tf_op jit(solution)/shard_map/ppermute | solution.py:272
  22.3 17.9 %collective-permute-start.8 = (bf16[2,144,256]{2,1,0:T(8,128)(2,1)S(1)}, bf16[2,144,256]{2,1,0:T(8,128)(2,1)S(1)}, u32[]{:S(2)}, u32[]{:S(2)}) collective-permute-start(bf16[2,144,256]{2,1,0:T(8,128)(2,1)S(1)} %get-tuple-element.20), channel_id=1, source_target_pairs={{0,3},{1,2},{2,1},{3,0},{4,7},{5,6},{6,5},{7,4},{8,11},{9,10},{10,... | collective-permute-start | bytes 442376 | tf_op jit(solution)/shard_map/ppermute | solution.py:272
  26.8 13.4 %collective-permute-start.9 = (bf16[2,144,256]{2,1,0:T(8,128)(2,1)S(1)}, bf16[2,144,256]{2,1,0:T(8,128)(2,1)S(1)}, u32[]{:S(2)}, u32[]{:S(2)}) collective-permute-start(bf16[2,144,256]{2,1,0:T(8,128)(2,1)S(1)} %get-tuple-element.22), channel_id=1, source_target_pairs={{0,1},{1,0},{2,3},{3,2},{4,5},{5,4},{6,7},{7,6},{8,9},{9,8},{10,11... | collective-permute-start | bytes 442376 | tf_op jit(solution)/shard_map/ppermute | solution.py:272
  28.5 11.8 %collective-permute-start.10 = (bf16[2,144,256]{2,1,0:T(8,128)(2,1)S(1)}, bf16[2,144,256]{2,1,0:T(8,128)(2,1)S(1)}, u32[]{:S(2)}, u32[]{:S(2)}) collective-permute-start(bf16[2,144,256]{2,1,0:T(8,128)(2,1)S(1)} %get-tuple-element.23), channel_id=1, source_target_pairs={{0,2},{1,3},{2,0},{3,1},{4,6},{5,7},{6,4},{7,5},{8,10},{9,11},{10,... | collective-permute-start | bytes 442376 | tf_op jit(solution)/shard_map/ppermute | solution.py:272
  29.1 11.1 %collective-permute-start.11 = (bf16[2,144,256]{2,1,0:T(8,128)(2,1)S(1)}, bf16[2,144,256]{2,1,0:T(8,128)(2,1)S(1)}, u32[]{:S(2)}, u32[]{:S(2)}) collective-permute-start(bf16[2,144,256]{2,1,0:T(8,128)(2,1)S(1)} %get-tuple-element.24), channel_id=1, source_target_pairs={{0,3},{1,2},{2,1},{3,0},{4,7},{5,6},{6,5},{7,4},{8,11},{9,10},{10,... | collective-permute-start | bytes 442376 | tf_op jit(solution)/shard_map/ppermute | solution.py:272

commit v2 on v0

v2 whole, which is shorter than its diff:
```python
import jax
import jax.numpy as jnp
from jax import lax
from jax.experimental import pallas as pl
from jax.experimental.pallas import tpu as pltpu
from jax.sharding import PartitionSpec as P

CAP = 2
LANES = 128
PAD = 16
BF, F32, I32 = jnp.bfloat16, jnp.float32, jnp.int32
VM = pl.BlockSpec(memory_space=pltpu.VMEM)
SM = pl.BlockSpec(memory_space=pltpu.SMEM)


def call(body, outs, ins, out_specs=None, scratch=(), us=1.0, limit=40):
    return pl.pallas_call(
        body,
        out_shape=outs,
        in_specs=ins,
        out_specs=out_specs or [VM] * len(outs),
        scratch_shapes=list(scratch),
        compiler_params=pltpu.CompilerParams(vmem_limit_bytes=limit * 2**20),
        cost_estimate=pl.CostEstimate(flops=int(us * 10**9), bytes_accessed=1000, transcendentals=0),
    )


def dot(x, y):
    return jnp.dot(x, y, preferred_element_type=F32)


def iota(shape, dim):
    return lax.broadcasted_iota(I32, shape, dim)


def zero_one(mask):
    return mask.astype(F32).astype(BF)


def rows_apart(x, atoms):
    block = x.shape[0] // atoms
    size = block // 2
    to, of = iota((block, block), 0), iota((block, block), 1)
    pick = zero_one(of == jnp.where(to < size, 2 * to, 2 * (to - size) + 1))
    wide = jnp.concatenate([x[a * block : (a + 1) * block] for a in range(atoms)], axis=1)
    return dot(pick, wide).astype(BF)


def convolve_kernel(shifts, weights, x, beyond, out):
    atoms, size, wide = out.shape
    span = wide // 2
    gap = iota((2 * span, span), 0) - iota((2 * span, span), 1)
    band = jnp.zeros(gap.shape, F32)
    for q in range(shifts.shape[0]):
        band = band + jnp.where(gap == shifts[q], weights[q], 0.0)
    high = band.astype(BF)
    low = (band - high.astype(F32)).astype(BF)
    parts = rows_apart(x[...], atoms), rows_apart(beyond[...], atoms)
    for a in range(atoms):
        z = jnp.concatenate([y[:, a * span : (a + 1) * span] for y in parts], axis=1)
        y = (dot(z, high) + dot(z, low)).astype(BF)
        out[a] = jnp.concatenate([y[:size], y[size:]], axis=1)


def plan_kernel(names, table, target):
    atoms, nbr = names.shape
    devices = table.shape[0]
    me = lax.axis_index("atom")
    device = iota((devices, nbr), 0)
    ahead = zero_one(iota((nbr, nbr), 0) < iota((nbr, nbr), 1))
    lane = iota(table.shape, 1)
    found = jnp.zeros(table.shape, F32)
    seen = jnp.zeros((devices, 1), F32)
    for a in range(atoms):
        entry = names[a : a + 1, :]
        owner = lax.div(entry, atoms)
        row = entry - owner * atoms
        match = (jnp.broadcast_to(owner, (devices, nbr)) == device).astype(F32)
        rank = dot(match.astype(BF), ahead) + seen
        seen = seen + jnp.sum(match, axis=1, keepdims=True)
        rows = jnp.broadcast_to(row, (devices, nbr)).astype(F32)
        for r in range(CAP):
            here = jnp.where(rank == r, match, 0.0)
            found = found + jnp.where(lane == r, jnp.sum(here * rows, axis=1, keepdims=True), 0.0)
            if a:
                found = found + jnp.where(lane == CAP + r, a * jnp.sum(here, axis=1, keepdims=True), 0.0)
        own_rank = jnp.minimum(jnp.sum(match * rank, axis=0, keepdims=True), CAP - 1.0).astype(I32)
        target[a : a + 1, :] = jnp.where(owner == me, row * atoms + a, atoms * atoms + owner * CAP + own_rank)
    table[...] = found.astype(I32)


def make_fetch(mates, over):
    def kernel(*refs):
        tables, unit, outs = refs[:mates], refs[mates], refs[-mates:]
        holder = lax.bitwise_xor(lax.axis_index("atom"), over)
        for table, out in zip(tables, outs):
            for r in range(CAP):
                out[r] = unit[table[holder, r]]

    return kernel


def make_form(orb):
    size = orb * orb
    tail = size - LANES
    reps = LANES // tail
    groups = pl.cdiv(orb, reps)
    height = (orb + groups) * PAD

    def kernel(target, x, ops, left, right, sums):
        atoms, nbr = target.shape
        terms = x.shape[0]
        slots = ops.shape[0]
        dirs = terms // (atoms * nbr)
        source, lane = iota((size, LANES), 0), iota((size, LANES), 1)

        def spread(at):
            group = sum(((at >= m * orb).astype(I32) for m in range(1, orb)), jnp.zeros(at.shape, I32))
            return group, at - group * orb

        group, within = spread(lane)
        tail_group, tail_within = spread(LANES + lax.bitwise_and(lane, tail - 1))
        part = lax.shift_right_logical(lane, tail.bit_length() - 1)
        values = x[...]
        left_at, tail_at = source - group, source - part * orb - tail_group
        for i in range(orb):
            left[i] = dot(values, zero_one(left_at == i * orb)).astype(BF)
        for g in range(groups):
            left[orb + g] = dot(values, zero_one(tail_at == g * reps * orb)).astype(BF)
        right_at, tail_right = source - within, source - tail_within
        for f in range(orb):
            right[0, f] = dot(values, zero_one(right_at == f * orb)).astype(BF)
            right[1, f] = dot(values, zero_one(tail_right == f * orb)).astype(BF)
        behind = iota((nbr, terms), 1) - iota((nbr, terms), 0) * dirs
        mask = jnp.zeros((slots, terms), F32)
        for a in range(atoms):
            hit = zero_one(jnp.broadcast_to(target[a : a + 1, :], (slots, nbr)) == iota((slots, nbr), 0))
            shifted = behind - a * nbr * dirs
            mask = mask + dot(hit, zero_one((shifted >= 0) & (shifted < dirs)))
        mask = mask.astype(BF)
        for i in range(orb + groups):
            c = i // orb
            lhs = left[i]
            for f in range(0, orb, 2):
                pair = [lhs * right[c, f + m] for m in range(2)]
                found = dot(mask, jnp.concatenate(pair, axis=1))
                for m in range(2):
                    sums[pl.ds(i * PAD + f + m, slots, stride=height), :] = found[:, m * LANES : (m + 1) * LANES]
        at = lax.shift_right_logical(iota((PAD, LANES), 1), tail.bit_length() - 1)
        real = iota((PAD, LANES), 0) < orb

        def settle(slot, carry):
            base = slot * height

            def tile(i):
                return jnp.where(real, sums[pl.ds(pl.multiple_of(base + i * PAD, PAD), PAD), :], 0.0)

            packed = [tile(orb + g) for g in range(groups)]
            for i in range(orb):
                ops[slot, i * PAD : (i + 1) * PAD, :LANES] = tile(i).astype(BF)
                ops[slot, i * PAD : (i + 1) * PAD, LANES:] = jnp.where(at == i % reps, packed[i // reps], 0.0).astype(BF)
            return carry

        lax.fori_loop(0, slots, settle, 0, unroll=2)

    return kernel


def tall(block):
    tail = block.shape[0] - LANES
    return jnp.concatenate([block[:LANES]] + [block[LANES:]] * (LANES // tail), axis=0)


def make_local(mates, half):
    def kernel(*refs):
        table, ops = refs[:2]
        own, mirror = refs[2:4]
        near, total = refs[4 : 4 + mates], refs[-1]
        atoms, height, wide = total.shape
        me = lax.axis_index("atom")
        run = jnp.zeros((atoms * height, wide), F32)
        for b in range(atoms):
            block = tall(own[b])
            lhs = ops[b * atoms : (b + 1) * atoms].reshape(atoms * height, ops.shape[2])
            run = run + dot(lhs, block)
        total[...] = run.reshape(total.shape)
        for s in range(mates):
            for r in range(CAP):
                owner = lax.bitwise_xor(me, s + 1)
                total[table[owner, CAP + r]] += dot(ops[atoms * atoms + owner * CAP + r], tall(near[s][r]))
        for r in range(CAP):
            owner = lax.bitwise_xor(me, half)
            block = tall(mirror[table[owner, r]])
            total[table[owner, CAP + r]] += dot(ops[atoms * atoms + owner * CAP + r], block)

    return kernel


def make_final(mates, half, orb):
    size = orb * orb

    def kernel(*refs):
        table, ops, begun = refs[:3]
        far, out, total = refs[3 : 3 + mates], refs[-2], refs[-1]
        atoms, height, wide = total.shape
        span = wide // 2
        me = lax.axis_index("atom")
        total[...] = begun[...]
        for s in range(mates):
            for r in range(CAP):
                owner = lax.bitwise_xor(me, half + s + 1)
                total[table[owner, CAP + r]] += dot(ops[atoms * atoms + owner * CAP + r], tall(far[s][r]))

        to, of = iota((2 * size, height), 0), iota((2 * size, height), 1)
        f = lax.bitwise_and(of, PAD - 1)
        at = 2 * (lax.shift_right_logical(of, PAD.bit_length() - 1) * orb + f)
        even = zero_one((to == at) & (f < orb))
        odd = zero_one((to == at + 1) & (f < orb))
        parts = [[total[a, :, p * span : (p + 1) * span].astype(BF) for a in range(atoms)] for p in range(2)]
        rows = dot(even, jnp.concatenate(parts[0], axis=1)) + dot(odd, jnp.concatenate(parts[1], axis=1))
        for a in range(atoms):
            out[a * 2 * size : (a + 1) * 2 * size, :] = rows[:, a * span : (a + 1) * span].astype(BF)

    return kernel


def on_device(green, coupling, neighbours, shifts, weights):
    atoms, _, orb, _, span = green.shape
    size = orb * orb
    devices = lax.axis_size("atom")
    half = devices // 2
    mates = half - 1
    peers = lax.axis_size("energy")
    shape = jax.ShapeDtypeStruct

    def across(value, by):
        return lax.ppermute(value, "atom", [(i, i ^ by) for i in range(devices)])

    x = green.transpose(0, 2, 3, 1, 4).reshape(atoms * size * 2, span)
    beyond = lax.ppermute(x, "energy", [(i, i - 1) for i in range(1, peers)])
    table, target = call(
        plan_kernel, [shape((devices, LANES), I32), shape(neighbours.shape, I32)], [VM], us=3.0
    )(neighbours)
    tables = [across(table, s) for s in range(1, half)]
    (unit,) = call(convolve_kernel, [shape((atoms, size, 2 * span), BF)], [SM, SM, VM, VM], us=1.5)(
        shifts, weights, x, beyond
    )
    mirror = across(unit, half)
    pair = shape((CAP, size, 2 * span), BF)
    own_out = call(make_fetch(mates, 0), [pair] * mates, [SM] * mates + [VM])(*tables, unit)
    near = [across(v, s + 1) for s, v in enumerate(own_out)]

    terms = coupling.reshape(-1, size)
    height, groups = orb * PAD, pl.cdiv(orb, LANES // (size - LANES))
    slots = atoms * atoms + devices * CAP
    (ops,) = call(
        make_form(orb),
        [shape((slots, height, 2 * LANES), BF)],
        [VM, VM],
        None,
        [
            pltpu.VMEM((orb + groups, terms.shape[0], LANES), BF),
            pltpu.VMEM((2, orb, terms.shape[0], LANES), BF),
            pltpu.VMEM((slots * (height + groups * PAD), LANES), F32),
        ],
        us=5.0,
    )(target, terms)

    relay_out = call(
        make_fetch(mates, half), [pair] * mates, [SM] * mates + [VM, pl.BlockSpec(memory_space=pl.ANY)]
    )(*tables, mirror, ops)
    far = [across(v, s + 1) for s, v in enumerate(relay_out)]
    total = shape((atoms, height, 2 * span), F32)
    (begun,) = call(make_local(mates, half), [total], [SM] + [VM] * (3 + mates), us=2.0)(
        table, ops, unit, mirror, *near
    )
    (out,) = call(
        make_final(mates, half, orb),
        [shape(x.shape, BF)],
        [SM] + [VM] * (2 + mates),
        None,
        [pltpu.VMEM(total.shape, F32)],
    )(table, ops, begun, *far)
    return out.reshape(atoms, orb, orb, 2, span).transpose(0, 3, 1, 2, 4)


def solution(mesh):
    placed = (P("atom", None, None, None, "energy"), P("atom", None), P("atom", None), P(), P())
    return jax.shard_map(
        on_device,
        mesh=mesh,
        in_specs=placed,
        out_specs=P("atom", None, None, None, "energy"),
        check_vma=False,
    )
```

time: 88.5 us -> 39 us (0.44); the launches traced: 87.2 us -> 38.8 us
  waiting for transfers between devices: 31.1 us -> 8.67 us
  local copies, waits for them, and re-layouts: 22.5 us -> 0.93 us
  matrix products: 15 us -> 0 us
  Pallas kernels: 0 us -> 12.6 us
  other arithmetic: 6.14 us -> 0 us
  starting transfers between devices: 12.3 us -> 16.5 us
    all_to_all x2 -> x0, waiting for transfers between devices: 31.1 us -> none  [the longest x1 27.6 us: on_device(): lax.all_to_all(outgoing, 'atom', split_axis=0, concat_axis=0, tiled=True)]
    ppermute x1 -> x11, starting transfers between devices: 1.28 us -> 16.5 us  [the longest x10 15.1 us: across(): return lax.ppermute(value, 'atom', [(i, i ^ by) for i in range(devices)])]
    dot_general x10 -> x0, matrix products: 15 us -> none  [the longest x4 7.88 us: couple_sum(): jnp.einsum('kdab,kpbce->kdpace', matrices, blocks, preferred_element_type...]
    pallas_call x0 -> x7, Pallas kernels: none -> 12.6 us  [the longest x1 5.86 us: on_device(): call(make_form(orb), [shape((slots, height, 2 * LANES), BF)], [VM, VM], N...]
    gather x5 -> x0, local copies, waits for them, and re-layouts: 11 us -> none  [the longest x4 10.2 us: one_atom(): return couple_sum(packed[0], table[packed[1]])]
    all_to_all x2 -> x0, starting transfers between devices: 11 us -> none  [the longest x1 7.28 us: on_device(): lax.all_to_all(request.reshape(device_count, capacity), 'atom', split_axi...]
    ppermute x1 -> x11, waiting for transfers between devices: 0.01 us -> 8.67 us  [the longest x10 8.67 us: across(): return lax.ppermute(value, 'atom', [(i, i ^ by) for i in range(devices)])]
    reshape x8 -> x1, local copies, waits for them, and re-layouts: 6.37 us -> 0.24 us  [on_device(): terms = coupling.reshape(-1, size)]
  transfers between devices with their start and end apart: 3 -> 11, of which waited for: 2 -> 4; matrix products, arithmetic and copies ran while one was open for 5% -> 1% of each run, Pallas kernels for 0% -> 27%
where the time goes in v2:
time: 39 us; the launch traced here: 38.8 us
  starting transfers between devices  16.5 us (42%)
  Pallas kernels  12.6 us (32%)
  waiting for transfers between devices  8.67 us (22%)
  local copies, waits for them, and re-layouts  0.93 us (2%)
    ppermute x10, starting transfers between devices, across(): return lax.ppermute(value, 'atom', [(i, i ^ by) for i in range(devices)])  15.1 us
    ppermute x10, waiting for transfers between devices, across(): return lax.ppermute(value, 'atom', [(i, i ^ by) for i in range(devices)])  8.67 us
    pallas_call x1, Pallas kernels, on_device(): call(make_form(orb), [shape((slots, height, 2 * LANES), BF)], [VM, VM], N...  5.86 us
    pallas_call x1, Pallas kernels, on_device(): call(make_final(mates, half, orb), [shape(x.shape, BF)], [SM] + [VM] * (2...  1.96 us
    pallas_call x1, Pallas kernels, on_device(): call(make_local(mates, half), [total], [SM] + [VM] * (3 + mates), us=2.0)  1.56 us
    pallas_call x1, Pallas kernels, on_device(): call(convolve_kernel, [shape((atoms, size, 2 * span), BF)], [SM, SM, VM,...  1.47 us
    ppermute x1, starting transfers between devices, on_device(): beyond = lax.ppermute(x, 'energy', [(i, i - 1) for i in range(1, peers)])  1.41 us
  transfers between devices with their start and end apart: 11, of which 4 were waited for; matrix products, arithmetic and copies ran while one was open for 1% of the time, Pallas kernels for 27%

profile of v2, /device:TPU:0, one launch (start us, length us, event | category | flops | bytes accessed | tf_op | source)
XLA Modules:
  0.0 38.8 jit_solution(8608407884852117582)
XLA Ops:
  0.0 1.4 %collective-permute-start = (bf16[1152,128]{1,0:T(8,128)(2,1)}, bf16[1152,128]{1,0:T(8,128)(2,1)S(1)}, u32[]{:S(2)}, u32[]{:S(2)}) collective-permute-start(bf16[1152,128]{1,0:T(8,128)(2,1)} %bitcast.6), channel_id=1, source_target_pairs={{8,0},{16,8},{24,16},{9,1},{17,9},{25,17},{10,2},{18,10},{26,18},{... | collective-permute-start | bytes 884744 | tf_op jit(solution)/shard_map/ppermute | solution.py:240
  1.4 0.7 %copy-done.1 = s32[4,24]{1,0:T(4,128)S(1)} copy-done((s32[4,24]{1,0:T(4,128)S(1)}, s32[4,24]{1,0:T(4,128)}, u32[]{:S(2)}) %copy-start.1) | copy-done | bytes 408
  2.1 0.2 shard_map.55
  2.3 4.0 %collective-permute-start.4 = (s32[8,128]{1,0:T(8,128)S(1)}, s32[8,128]{1,0:T(8,128)S(1)}, u32[]{:S(2)}, u32[]{:S(2)}) collective-permute-start(s32[8,128]{1,0:T(8,128)S(1)} %get-tuple-element.13.refs_0_), channel_id=1, source_target_pairs={{0,3},{1,2},{2,1},{3,0},{4,7},{5,6},{6,5},{7,4},{8,11},{9,10},{10,... | collective-permute-start | bytes 12296 | tf_op jit(solution)/shard_map/ppermute | solution.py:237
  6.4 0.4 %collective-permute-start.3 = (s32[8,128]{1,0:T(8,128)S(1)}, s32[8,128]{1,0:T(8,128)S(1)}, u32[]{:S(2)}, u32[]{:S(2)}) collective-permute-start(s32[8,128]{1,0:T(8,128)S(1)} %get-tuple-element.13.refs_0_), channel_id=1, source_target_pairs={{0,2},{1,3},{2,0},{3,1},{4,6},{5,7},{6,4},{7,5},{8,10},{9,11},{10,... | collective-permute-start | bytes 12296 | tf_op jit(solution)/shard_map/ppermute | solution.py:237
  6.8 0.2 collective-permute-start.2
  7.0 0.2 reshape.9.x
  7.3 1.5 %shard_map.57.refs_3_.refs_2_ = bf16[4,144,256]{2,1,0:T(8,128)(2,1)S(1)} custom-call(s32[16]{0:T(128)S(1)} %copy-done.2, f32[16]{0:T(128)S(1)} %copy-done.3, bf16[1152,128]{1,0:T(8,128)(2,1)S(1)} %bitcast.7, bf16[1152,128]{1,0:T(8,128)(2,1)S(1)} %collective-permute-done.beyond), custom_call_target="tpu_custom_call" | custom-call | flops 1500000000 | bytes 1000 | tf_op jit(solution)/shard_map/pallas_call | solution.py:245
  8.8 3.0 %collective-permute-start.1 = (bf16[4,144,256]{2,1,0:T(8,128)(2,1)S(1)}, bf16[4,144,256]{2,1,0:T(8,128)(2,1)S(1)}, u32[]{:S(2)}, u32[]{:S(2)}) collective-permute-start(bf16[4,144,256]{2,1,0:T(8,128)(2,1)S(1)} %shard_map.57.refs_3_.refs_2_), channel_id=1, source_target_pairs={{0,4},{1,5},{2,6},{3,7},{4,0},{5,1},{6,2},{7,3},{8,12},{9,13},{10,... | collective-permute-start | bytes 884744 | tf_op jit(solution)/shard_map/ppermute | solution.py:237
  11.8 0.8 %shard_map.58 = (bf16[2,144,256]{2,1,0:T(8,128)(2,1)S(1)}, bf16[2,144,256]{2,1,0:T(8,128)(2,1)S(1)}, bf16[2,144,256]{2,1,0:T(8,128)(2,1)S(1)}) custom-call(s32[8,128]{1,0:T(8,128)S(1)} %collective-permute-done.2.refs_0_, s32[8,128]{1,0:T(8,128)S(1)} %collective-permute-done.3.refs_1_, s32[8,128]{1,0:T(8,128)S(1)} %collective-permute-done.4.refs_2_, ...), custom_call_target="tpu_custom_call" | custom-call | flops 1000000000 | bytes 1000 | tf_op jit(solution)/shard_map/pallas_call | solution.py:250
  12.6 1.6 %collective-permute-start.5 = (bf16[2,144,256]{2,1,0:T(8,128)(2,1)S(1)}, bf16[2,144,256]{2,1,0:T(8,128)(2,1)S(1)}, u32[]{:S(2)}, u32[]{:S(2)}) collective-permute-start(bf16[2,144,256]{2,1,0:T(8,128)(2,1)S(1)} %get-tuple-element.15), channel_id=1, source_target_pairs={{0,1},{1,0},{2,3},{3,2},{4,5},{5,4},{6,7},{7,6},{8,9},{9,8},{10,11... | collective-permute-start | bytes 442376 | tf_op jit(solution)/shard_map/ppermute | solution.py:237
  14.1 1.6 %collective-permute-start.6 = (bf16[2,144,256]{2,1,0:T(8,128)(2,1)S(1)}, bf16[2,144,256]{2,1,0:T(8,128)(2,1)S(1)}, u32[]{:S(2)}, u32[]{:S(2)}) collective-permute-start(bf16[2,144,256]{2,1,0:T(8,128)(2,1)S(1)} %get-tuple-element.16), channel_id=1, source_target_pairs={{0,2},{1,3},{2,0},{3,1},{4,6},{5,7},{6,4},{7,5},{8,10},{9,11},{10,... | collective-permute-start | bytes 442376 | tf_op jit(solution)/shard_map/ppermute | solution.py:237
  15.7 0.4 %collective-permute-start.7 = (bf16[2,144,256]{2,1,0:T(8,128)(2,1)S(1)}, bf16[2,144,256]{2,1,0:T(8,128)(2,1)S(1)}, u32[]{:S(2)}, u32[]{:S(2)}) collective-permute-start(bf16[2,144,256]{2,1,0:T(8,128)(2,1)S(1)} %get-tuple-element.17), channel_id=1, source_target_pairs={{0,3},{1,2},{2,1},{3,0},{4,7},{5,6},{6,5},{7,4},{8,11},{9,10},{10,... | collective-permute-start | bytes 442376 | tf_op jit(solution)/shard_map/ppermute | solution.py:237
  16.1 5.9 %shard_map.56.refs_1_.refs_4_ = bf16[32,192,256]{2,1,0:T(8,128)(2,1)S(1)} custom-call(s32[4,24]{1,0:T(4,128)S(1)} %get-tuple-element.14.target, bf16[288,144]{1,0:T(8,128)(2,1)S(1)} %reshape.9.x), custom_call_target="tpu_custom_call" | custom-call | flops 5000000000 | bytes 1000 | tf_op jit(solution)/shard_map/pallas_call | solution.py:256
  22.0 2.6 %collective-permute-done.1.refs_3_ = bf16[4,144,256]{2,1,0:T(8,128)(2,1)S(1)} collective-permute-done((bf16[4,144,256]{2,1,0:T(8,128)(2,1)S(1)}, bf16[4,144,256]{2,1,0:T(8,128)(2,1)S(1)}, u32[]{:S(2)}, u32[]{:S(2)}) %collective-permute-start.1) | collective-permute-done | bytes 294944 | tf_op jit(solution)/shard_map/ppermute | solution.py:237
  24.6 0.8 %shard_map.60 = (bf16[2,144,256]{2,1,0:T(8,128)(2,1)S(1)}, bf16[2,144,256]{2,1,0:T(8,128)(2,1)S(1)}, bf16[2,144,256]{2,1,0:T(8,128)(2,1)S(1)}) custom-call(s32[8,128]{1,0:T(8,128)S(1)} %collective-permute-done.2.refs_0_, s32[8,128]{1,0:T(8,128)S(1)} %collective-permute-done.3.refs_1_, s32[8,128]{1,0:T(8,128)S(1)} %collective-permute-done.4.refs_2_, ...), custom_call_target="tpu_custom_call" | custom-call | flops 1000000000 | bytes 1000 | tf_op jit(solution)/shard_map/pallas_call | solution.py:269
  25.4 2.3 %collective-permute-start.8 = (bf16[2,144,256]{2,1,0:T(8,128)(2,1)S(1)}, bf16[2,144,256]{2,1,0:T(8,128)(2,1)S(1)}, u32[]{:S(2)}, u32[]{:S(2)}) collective-permute-start(bf16[2,144,256]{2,1,0:T(8,128)(2,1)S(1)} %get-tuple-element.18), channel_id=1, source_target_pairs={{0,1},{1,0},{2,3},{3,2},{4,5},{5,4},{6,7},{7,6},{8,9},{9,8},{10,11... | collective-permute-start | bytes 442376 | tf_op jit(solution)/shard_map/ppermute | solution.py:237
  27.6 1.6 %collective-permute-start.9 = (bf16[2,144,256]{2,1,0:T(8,128)(2,1)S(1)}, bf16[2,144,256]{2,1,0:T(8,128)(2,1)S(1)}, u32[]{:S(2)}, u32[]{:S(2)}) collective-permute-start(bf16[2,144,256]{2,1,0:T(8,128)(2,1)S(1)} %get-tuple-element.19), channel_id=1, source_target_pairs={{0,2},{1,3},{2,0},{3,1},{4,6},{5,7},{6,4},{7,5},{8,10},{9,11},{10,... | collective-permute-start | bytes 442376 | tf_op jit(solution)/shard_map/ppermute | solution.py:237
  29.3 0.0 collective-permute-done.5.refs_4_
  29.3 1.6 %shard_map.59.refs_2_ = f32[4,192,256]{2,1,0:T(8,128)S(1)} custom-call(s32[8,128]{1,0:T(8,128)S(1)} %get-tuple-element.13.refs_0_, bf16[32,192,256]{2,1,0:T(8,128)(2,1)S(1)} %shard_map.56.refs_1_.refs_4_, bf16[4,144,256]{2,1,0:T(8,128)(2,1)S(1)} %shard_map.57.refs_3_.refs_2_, bf16[4,144,256]{2,1,0:T(8,128)(2,1)S(1)} %collective-permute-done.1.refs_3_, ...), custom_call_target="tpu_custom_call" | custom-call | flops 2000000000 | bytes 1000 | tf_op jit(solution)/shard_map/pallas_call | solution.py:274
  30.8 1.1 %collective-permute-done.8.refs_3_ = bf16[2,144,256]{2,1,0:T(8,128)(2,1)S(1)} collective-permute-done((bf16[2,144,256]{2,1,0:T(8,128)(2,1)S(1)}, bf16[2,144,256]{2,1,0:T(8,128)(2,1)S(1)}, u32[]{:S(2)}, u32[]{:S(2)}) %collective-permute-start.8) | collective-permute-done | bytes 147488 | tf_op jit(solution)/shard_map/ppermute | solution.py:237
  31.9 2.4 %collective-permute-done.9.refs_4_ = bf16[2,144,256]{2,1,0:T(8,128)(2,1)S(1)} collective-permute-done((bf16[2,144,256]{2,1,0:T(8,128)(2,1)S(1)}, bf16[2,144,256]{2,1,0:T(8,128)(2,1)S(1)}, u32[]{:S(2)}, u32[]{:S(2)}) %collective-permute-start.9) | collective-permute-done | bytes 147488 | tf_op jit(solution)/shard_map/ppermute | solution.py:237
  34.3 2.5 %collective-permute-done.10.refs_5_ = bf16[2,144,256]{2,1,0:T(8,128)(2,1)S(1)} collective-permute-done((bf16[2,144,256]{2,1,0:T(8,128)(2,1)S(1)}, bf16[2,144,256]{2,1,0:T(8,128)(2,1)S(1)}, u32[]{:S(2)}, u32[]{:S(2)}) %collective-permute-start.10) | collective-permute-done | bytes 147488 | tf_op jit(solution)/shard_map/ppermute | solution.py:237
  36.9 2.0 %shard_map.61 = bf16[1152,128]{1,0:T(8,128)(2,1)} custom-call(s32[8,128]{1,0:T(8,128)S(1)} %get-tuple-element.13.refs_0_, bf16[32,192,256]{2,1,0:T(8,128)(2,1)S(1)} %shard_map.56.refs_1_.refs_4_, f32[4,192,256]{2,1,0:T(8,128)S(1)} %shard_map.59.refs_2_, bf16[2,144,256]{2,1,0:T(8,128)(2,1)S(1)} %collective-permute-done.8.refs_3_, ...), custom_call_target="tpu_custom_call" | custom-call | flops 1000000000 | bytes 1000 | tf_op jit(solution)/shard_map/pallas_call | solution.py:277
  (16 shorter events, 0.0 us)
Async XLA Ops:
  0.0 7.3 %copy-start = (bf16[4,2,12,12,128]{4,1,3,2,0:T(2,128)(2,1)S(1)}, bf16[4,2,12,12,128]{4,1,3,2,0:T(2,128)(2,1)}, u32[]{:S(2)}) copy-start(bf16[4,2,12,12,128]{4,1,3,2,0:T(2,128)(2,1)} %param.5) | copy-start | bytes 884740
  0.0 7.3 %collective-permute-start = (bf16[1152,128]{1,0:T(8,128)(2,1)}, bf16[1152,128]{1,0:T(8,128)(2,1)S(1)}, u32[]{:S(2)}, u32[]{:S(2)}) collective-permute-start(bf16[1152,128]{1,0:T(8,128)(2,1)} %bitcast.6), channel_id=1, source_target_pairs={{8,0},{16,8},{24,16},{9,1},{17,9},{25,17},{10,2},{18,10},{26,18},{... | collective-permute-start | bytes 884744 | tf_op jit(solution)/shard_map/ppermute | solution.py:240
  1.4 0.7 %copy-start.1 = (s32[4,24]{1,0:T(4,128)S(1)}, s32[4,24]{1,0:T(4,128)}, u32[]{:S(2)}) copy-start(s32[4,24]{1,0:T(4,128)} %names.1) | copy-start | bytes 1156
  2.1 4.9 %copy-start.4 = (bf16[4,10368]{1,0:T(4,128)(2,1)S(1)}, bf16[4,10368]{1,0:T(4,128)(2,1)}, u32[]{:S(2)}) copy-start(bf16[4,10368]{1,0:T(4,128)(2,1)} %param.6) | copy-start | bytes 248836
  2.1 5.2 %copy-start.2 = (s32[16]{0:T(128)S(1)}, s32[16]{0:T(128)}, u32[]{:S(2)}) copy-start(s32[16]{0:T(128)} %shifts.1) | copy-start | bytes 196
  2.1 5.2 %copy-start.3 = (f32[16]{0:T(128)S(1)}, f32[16]{0:T(128)}, u32[]{:S(2)}) copy-start(f32[16]{0:T(128)} %weights.1) | copy-start | bytes 196
  2.3 9.4 %collective-permute-start.4 = (s32[8,128]{1,0:T(8,128)S(1)}, s32[8,128]{1,0:T(8,128)S(1)}, u32[]{:S(2)}, u32[]{:S(2)}) collective-permute-start(s32[8,128]{1,0:T(8,128)S(1)} %get-tuple-element.13.refs_0_), channel_id=1, source_target_pairs={{0,3},{1,2},{2,1},{3,0},{4,7},{5,6},{6,5},{7,4},{8,11},{9,10},{10,... | collective-permute-start | bytes 12296 | tf_op jit(solution)/shard_map/ppermute | solution.py:237
  6.4 5.4 %collective-permute-start.3 = (s32[8,128]{1,0:T(8,128)S(1)}, s32[8,128]{1,0:T(8,128)S(1)}, u32[]{:S(2)}, u32[]{:S(2)}) collective-permute-start(s32[8,128]{1,0:T(8,128)S(1)} %get-tuple-element.13.refs_0_), channel_id=1, source_target_pairs={{0,2},{1,3},{2,0},{3,1},{4,6},{5,7},{6,4},{7,5},{8,10},{9,11},{10,... | collective-permute-start | bytes 12296 | tf_op jit(solution)/shard_map/ppermute | solution.py:237
  6.8 4.9 %collective-permute-start.2 = (s32[8,128]{1,0:T(8,128)S(1)}, s32[8,128]{1,0:T(8,128)S(1)}, u32[]{:S(2)}, u32[]{:S(2)}) collective-permute-start(s32[8,128]{1,0:T(8,128)S(1)} %get-tuple-element.13.refs_0_), channel_id=1, source_target_pairs={{0,1},{1,0},{2,3},{3,2},{4,5},{5,4},{6,7},{7,6},{8,9},{9,8},{10,11... | collective-permute-start | bytes 12296 | tf_op jit(solution)/shard_map/ppermute | solution.py:237
  8.8 15.8 %collective-permute-start.1 = (bf16[4,144,256]{2,1,0:T(8,128)(2,1)S(1)}, bf16[4,144,256]{2,1,0:T(8,128)(2,1)S(1)}, u32[]{:S(2)}, u32[]{:S(2)}) collective-permute-start(bf16[4,144,256]{2,1,0:T(8,128)(2,1)S(1)} %shard_map.57.refs_3_.refs_2_), channel_id=1, source_target_pairs={{0,4},{1,5},{2,6},{3,7},{4,0},{5,1},{6,2},{7,3},{8,12},{9,13},{10,... | collective-permute-start | bytes 884744 | tf_op jit(solution)/shard_map/ppermute | solution.py:237
  12.6 16.7 %collective-permute-start.5 = (bf16[2,144,256]{2,1,0:T(8,128)(2,1)S(1)}, bf16[2,144,256]{2,1,0:T(8,128)(2,1)S(1)}, u32[]{:S(2)}, u32[]{:S(2)}) collective-permute-start(bf16[2,144,256]{2,1,0:T(8,128)(2,1)S(1)} %get-tuple-element.15), channel_id=1, source_target_pairs={{0,1},{1,0},{2,3},{3,2},{4,5},{5,4},{6,7},{7,6},{8,9},{9,8},{10,11... | collective-permute-start | bytes 442376 | tf_op jit(solution)/shard_map/ppermute | solution.py:237
  14.1 15.1 %collective-permute-start.6 = (bf16[2,144,256]{2,1,0:T(8,128)(2,1)S(1)}, bf16[2,144,256]{2,1,0:T(8,128)(2,1)S(1)}, u32[]{:S(2)}, u32[]{:S(2)}) collective-permute-start(bf16[2,144,256]{2,1,0:T(8,128)(2,1)S(1)} %get-tuple-element.16), channel_id=1, source_target_pairs={{0,2},{1,3},{2,0},{3,1},{4,6},{5,7},{6,4},{7,5},{8,10},{9,11},{10,... | collective-permute-start | bytes 442376 | tf_op jit(solution)/shard_map/ppermute | solution.py:237
  15.7 13.6 %collective-permute-start.7 = (bf16[2,144,256]{2,1,0:T(8,128)(2,1)S(1)}, bf16[2,144,256]{2,1,0:T(8,128)(2,1)S(1)}, u32[]{:S(2)}, u32[]{:S(2)}) collective-permute-start(bf16[2,144,256]{2,1,0:T(8,128)(2,1)S(1)} %get-tuple-element.17), channel_id=1, source_target_pairs={{0,3},{1,2},{2,1},{3,0},{4,7},{5,6},{6,5},{7,4},{8,11},{9,10},{10,... | collective-permute-start | bytes 442376 | tf_op jit(solution)/shard_map/ppermute | solution.py:237
  25.4 6.6 %collective-permute-start.8 = (bf16[2,144,256]{2,1,0:T(8,128)(2,1)S(1)}, bf16[2,144,256]{2,1,0:T(8,128)(2,1)S(1)}, u32[]{:S(2)}, u32[]{:S(2)}) collective-permute-start(bf16[2,144,256]{2,1,0:T(8,128)(2,1)S(1)} %get-tuple-element.18), channel_id=1, source_target_pairs={{0,1},{1,0},{2,3},{3,2},{4,5},{5,4},{6,7},{7,6},{8,9},{9,8},{10,11... | collective-permute-start | bytes 442376 | tf_op jit(solution)/shard_map/ppermute | solution.py:237
  27.6 6.7 %collective-permute-start.9 = (bf16[2,144,256]{2,1,0:T(8,128)(2,1)S(1)}, bf16[2,144,256]{2,1,0:T(8,128)(2,1)S(1)}, u32[]{:S(2)}, u32[]{:S(2)}) collective-permute-start(bf16[2,144,256]{2,1,0:T(8,128)(2,1)S(1)} %get-tuple-element.19), channel_id=1, source_target_pairs={{0,2},{1,3},{2,0},{3,1},{4,6},{5,7},{6,4},{7,5},{8,10},{9,11},{10,... | collective-permute-start | bytes 442376 | tf_op jit(solution)/shard_map/ppermute | solution.py:237
  29.3 7.6 %collective-permute-start.10 = (bf16[2,144,256]{2,1,0:T(8,128)(2,1)S(1)}, bf16[2,144,256]{2,1,0:T(8,128)(2,1)S(1)}, u32[]{:S(2)}, u32[]{:S(2)}) collective-permute-start(bf16[2,144,256]{2,1,0:T(8,128)(2,1)S(1)} %get-tuple-element.20), channel_id=1, source_target_pairs={{0,3},{1,2},{2,1},{3,0},{4,7},{5,6},{6,5},{7,4},{8,11},{9,10},{10,... | collective-permute-start | bytes 442376 | tf_op jit(solution)/shard_map/ppermute | solution.py:237

commit v3 on v2

--- a/solution.py
+++ b/solution.py
@@ -8,6 +8,7 @@
 CAP = 2
 LANES = 128
 PAD = 16
+SKEW = 8
 BF, F32, I32 = jnp.bfloat16, jnp.float32, jnp.int32
 VM = pl.BlockSpec(memory_space=pltpu.VMEM)
 SM = pl.BlockSpec(memory_space=pltpu.SMEM)
@@ -46,20 +47,43 @@
     return dot(pick, wide).astype(BF)
 
 
-def convolve_kernel(shifts, weights, x, beyond, out):
-    atoms, size, wide = out.shape
-    span = wide // 2
-    gap = iota((2 * span, span), 0) - iota((2 * span, span), 1)
+def beside(parts, atoms, span, size):
+    rows = []
+    for a in range(atoms):
+        lanes = [y[p * size : (p + 1) * size, a * span : (a + 1) * span] for p in range(2) for y in parts]
+        rows.append(jnp.concatenate(lanes, axis=1))
+    return jnp.concatenate(rows, axis=0)
+
+
+def low_kernel(spectrum, x, out, apart, bands):
+    atoms, size, span = out.shape
+    half = span // 2
+    lane = iota((2 * span, span), 1)
+    first = lane < half
+    gap = (iota((2 * span, span), 0) - half - jnp.where(first, lane, lane - half)).astype(F32)
     band = jnp.zeros(gap.shape, F32)
-    for q in range(shifts.shape[0]):
-        band = band + jnp.where(gap == shifts[q], weights[q], 0.0)
-    high = band.astype(BF)
-    low = (band - high.astype(F32)).astype(BF)
-    parts = rows_apart(x[...], atoms), rows_apart(beyond[...], atoms)
-    for a in range(atoms):
-        z = jnp.concatenate([y[:, a * span : (a + 1) * span] for y in parts], axis=1)
-        y = (dot(z, high) + dot(z, low)).astype(BF)
-        out[a] = jnp.concatenate([y[:size], y[size:]], axis=1)
+    for q in range(spectrum.shape[1]):
+        band = band + jnp.where(gap == spectrum[0, q], spectrum[1, q], 0.0)
+    rounded = band.astype(BF).astype(F32)
+
+    def parted(part, mask):
+        return jnp.concatenate([jnp.where(mask, part, 0.0), jnp.where(mask, 0.0, part)], axis=0).astype(BF)
+
+    bands[0] = parted(rounded, first)
+    bands[1] = parted(band - rounded, first)
+    y = rows_apart(x[...], atoms)
+    apart[...] = y
+    z = beside([y], atoms, span, size)
+    cut = slice(half, half + span)
+    y = dot(z, parted(rounded[cut], first[cut])) + dot(z, parted((band - rounded)[cut], first[cut]))
+    out[...] = y.astype(BF).reshape(out.shape)
+
+
+def high_kernel(apart, bands, beyond, out):
+    atoms, size, span = out.shape
+    z = beside([apart[...], rows_apart(beyond[...], atoms)], atoms, span, size)
+    y = dot(z, bands[0]) + dot(z, bands[1])
+    out[...] = y.astype(BF).reshape(out.shape)
 
 
 def plan_kernel(names, table, target):
@@ -89,13 +113,28 @@
     table[...] = found.astype(I32)
 
 
-def make_fetch(mates, over):
+def make_first(mates, half):
     def kernel(*refs):
-        tables, unit, outs = refs[:mates], refs[mates], refs[-mates:]
-        holder = lax.bitwise_xor(lax.axis_index("atom"), over)
+        tables, (low, high, mirror), outs = refs[:mates], refs[mates : mates + 3], refs[mates + 3 :]
+        span = low.shape[2]
+        me = lax.axis_index("atom")
         for table, out in zip(tables, outs):
             for r in range(CAP):
-                out[r] = unit[table[holder, r]]
+                row = table[me, r]
+                out[r, :, :span] = low[row]
+                out[r, :, span : 2 * span] = high[row]
+                out[r, :, 2 * span :] = mirror[table[lax.bitwise_xor(me, half), r]]
+
+    return kernel
+
+
+def make_second(mates, half):
+    def kernel(*refs):
+        tables, mirror, outs = refs[:mates], refs[mates], refs[mates + 1 :]
+        holder = lax.bitwise_xor(lax.axis_index("atom"), half)
+        for table, out in zip(tables, outs):
+            for r in range(CAP):
+                out[r] = mirror[table[holder, r]]
 
     return kernel
 
@@ -105,7 +144,7 @@
     tail = size - LANES
     reps = LANES // tail
     groups = pl.cdiv(orb, reps)
-    height = (orb + groups) * PAD
+    height = (orb + groups) * PAD + SKEW
 
     def kernel(target, x, ops, left, right, sums):
         atoms, nbr = target.shape
@@ -147,21 +186,21 @@
                 for m in range(2):
                     sums[pl.ds(i * PAD + f + m, slots, stride=height), :] = found[:, m * LANES : (m + 1) * LANES]
         at = lax.shift_right_logical(iota((PAD, LANES), 1), tail.bit_length() - 1)
-        real = iota((PAD, LANES), 0) < orb
+        only = [zero_one(at == m) for m in range(reps)]
 
         def settle(slot, carry):
             base = slot * height
 
             def tile(i):
-                return jnp.where(real, sums[pl.ds(pl.multiple_of(base + i * PAD, PAD), PAD), :], 0.0)
+                return sums[pl.ds(pl.multiple_of(base + i * PAD, PAD), PAD), :].astype(BF)
 
             packed = [tile(orb + g) for g in range(groups)]
             for i in range(orb):
-                ops[slot, i * PAD : (i + 1) * PAD, :LANES] = tile(i).astype(BF)
-                ops[slot, i * PAD : (i + 1) * PAD, LANES:] = jnp.where(at == i % reps, packed[i // reps], 0.0).astype(BF)
+                ops[slot, i * PAD : (i + 1) * PAD, :LANES] = tile(i)
+                ops[slot, i * PAD : (i + 1) * PAD, LANES:] = packed[i // reps] * only[i % reps]
             return carry
 
-        lax.fori_loop(0, slots, settle, 0, unroll=2)
+        lax.fori_loop(0, slots, settle, 0, unroll=4)
 
     return kernel
 
@@ -174,23 +213,24 @@
 def make_local(mates, half):
     def kernel(*refs):
         table, ops = refs[:2]
-        own, mirror = refs[2:4]
-        near, total = refs[4 : 4 + mates], refs[-1]
+        own, mirror = refs[2:4], refs[4:6]
+        near, total = refs[6 : 6 + mates], refs[-1]
         atoms, height, wide = total.shape
         me = lax.axis_index("atom")
         run = jnp.zeros((atoms * height, wide), F32)
         for b in range(atoms):
-            block = tall(own[b])
+            block = tall(jnp.concatenate([own[0][b], own[1][b]], axis=1))
             lhs = ops[b * atoms : (b + 1) * atoms].reshape(atoms * height, ops.shape[2])
             run = run + dot(lhs, block)
         total[...] = run.reshape(total.shape)
         for s in range(mates):
             for r in range(CAP):
-                owner = lax.bitwise_xor(me, s + 1)
-                total[table[owner, CAP + r]] += dot(ops[atoms * atoms + owner * CAP + r], tall(near[s][r]))
+                owner = lax.bitwise_xor(me, mates - s)
+                total[table[owner, CAP + r]] += dot(ops[atoms * atoms + owner * CAP + r], tall(near[s][r, :, :wide]))
         for r in range(CAP):
             owner = lax.bitwise_xor(me, half)
-            block = tall(mirror[table[owner, r]])
+            row = table[owner, r]
+            block = tall(jnp.concatenate([mirror[0][row], mirror[1][row]], axis=1))
             total[table[owner, CAP + r]] += dot(ops[atoms * atoms + owner * CAP + r], block)
 
     return kernel
@@ -201,27 +241,39 @@
 
     def kernel(*refs):
         table, ops, begun = refs[:3]
-        far, out, total = refs[3 : 3 + mates], refs[-2], refs[-1]
+        first, second = refs[3 : 3 + mates], refs[3 + mates : 3 + 2 * mates]
+        out, total = refs[-2:]
         atoms, height, wide = total.shape
         span = wide // 2
+        part = span // 2
         me = lax.axis_index("atom")
         total[...] = begun[...]
         for s in range(mates):
             for r in range(CAP):
-                owner = lax.bitwise_xor(me, half + s + 1)
-                total[table[owner, CAP + r]] += dot(ops[atoms * atoms + owner * CAP + r], tall(far[s][r]))
+                owner = lax.bitwise_xor(me, half + mates - s)
+                block = tall(jnp.concatenate([first[s][r, :, wide:], second[s][r]], axis=1))
+                total[table[owner, CAP + r]] += dot(ops[atoms * atoms + owner * CAP + r], block)
 
         to, of = iota((2 * size, height), 0), iota((2 * size, height), 1)
         f = lax.bitwise_and(of, PAD - 1)
         at = 2 * (lax.shift_right_logical(of, PAD.bit_length() - 1) * orb + f)
         even = zero_one((to == at) & (f < orb))
         odd = zero_one((to == at + 1) & (f < orb))
-        parts = [[total[a, :, p * span : (p + 1) * span].astype(BF) for a in range(atoms)] for p in range(2)]
+        real = lax.bitwise_and(iota((height, span), 0), PAD - 1) < orb
+        parts = [[], []]
+        for a in range(atoms):
+            for p in range(2):
+                lanes = [total[a, :, h * span + p * part : h * span + (p + 1) * part] for h in range(2)]
+                parts[p].append(jnp.where(real, jnp.concatenate(lanes, axis=1), 0.0).astype(BF))
         rows = dot(even, jnp.concatenate(parts[0], axis=1)) + dot(odd, jnp.concatenate(parts[1], axis=1))
         for a in range(atoms):
             out[a * 2 * size : (a + 1) * 2 * size, :] = rows[:, a * span : (a + 1) * span].astype(BF)
 
     return kernel
+
+
+def after(value, *earlier):
+    return lax.optimization_barrier((value,) + earlier)[0]
 
 
 def on_device(green, coupling, neighbours, shifts, weights):
@@ -237,18 +289,26 @@
         return lax.ppermute(value, "atom", [(i, i ^ by) for i in range(devices)])
 
     x = green.transpose(0, 2, 3, 1, 4).reshape(atoms * size * 2, span)
-    beyond = lax.ppermute(x, "energy", [(i, i - 1) for i in range(1, peers)])
-    table, target = call(
-        plan_kernel, [shape((devices, LANES), I32), shape(neighbours.shape, I32)], [VM], us=3.0
-    )(neighbours)
-    tables = [across(table, s) for s in range(1, half)]
-    (unit,) = call(convolve_kernel, [shape((atoms, size, 2 * span), BF)], [SM, SM, VM, VM], us=1.5)(
-        shifts, weights, x, beyond
+    spectrum = jnp.stack([shifts.astype(F32), weights])
+    unit = shape((atoms, size, span), BF)
+    low, apart, bands = call(
+        low_kernel,
+        [unit, shape((2 * size, atoms * span), BF), shape((2, 4 * span, span), BF)],
+        [SM, VM],
+        us=1.2,
+    )(spectrum, x)
+    beyond = lax.ppermute(after(x, low), "energy", [(i, i - 1) for i in range(1, peers)])
+    (high,) = call(high_kernel, [unit], [VM] * 3, us=0.7)(apart, bands, beyond)
+    mirror = across(low, half), across(high, half)
+    table, target = call(plan_kernel, [shape((devices, LANES), I32), shape(neighbours.shape, I32)], [VM], us=0.5)(
+        neighbours
     )
-    mirror = across(unit, half)
-    pair = shape((CAP, size, 2 * span), BF)
-    own_out = call(make_fetch(mates, 0), [pair] * mates, [SM] * mates + [VM])(*tables, unit)
-    near = [across(v, s + 1) for s, v in enumerate(own_out)]
+    tables = [across(after(table, high), s) for s in reversed(range(1, half))]
+    triple, single = shape((CAP, size, 3 * span), BF), shape((CAP, size, span), BF)
+    first_out = call(make_first(mates, half), [triple] * mates, [SM] * mates + [VM] * 3)(*tables, low, high, mirror[0])
+    near = [across(v, mates - s) for s, v in enumerate(first_out)]
+    second_out = call(make_second(mates, half), [single] * mates, [SM] * mates + [VM])(*tables, mirror[1])
+    far = [across(v, mates - s) for s, v in enumerate(second_out)]
 
     terms = coupling.reshape(-1, size)
     height, groups = orb * PAD, pl.cdiv(orb, LANES // (size - LANES))
@@ -261,26 +321,22 @@
         [
             pltpu.VMEM((orb + groups, terms.shape[0], LANES), BF),
             pltpu.VMEM((2, orb, terms.shape[0], LANES), BF),
-            pltpu.VMEM((slots * (height + groups * PAD), LANES), F32),
+            pltpu.VMEM(((slots + 1) * (height + groups * PAD + SKEW), LANES), F32),
         ],
-        us=5.0,
+        us=0.01,
     )(target, terms)
 
-    relay_out = call(
-        make_fetch(mates, half), [pair] * mates, [SM] * mates + [VM, pl.BlockSpec(memory_space=pl.ANY)]
-    )(*tables, mirror, ops)
-    far = [across(v, s + 1) for s, v in enumerate(relay_out)]
     total = shape((atoms, height, 2 * span), F32)
-    (begun,) = call(make_local(mates, half), [total], [SM] + [VM] * (3 + mates), us=2.0)(
-        table, ops, unit, mirror, *near
+    (begun,) = call(make_local(mates, half), [total], [SM] + [VM] * (5 + mates), us=1.5)(
+        table, ops, low, high, *mirror, *near
     )
     (out,) = call(
         make_final(mates, half, orb),
         [shape(x.shape, BF)],
-        [SM] + [VM] * (2 + mates),
+        [SM] + [VM] * (2 + 2 * mates),
         None,
         [pltpu.VMEM(total.shape, F32)],
-    )(table, ops, begun, *far)
+    )(table, ops, begun, *near, *far)
     return out.reshape(atoms, orb, orb, 2, span).transpose(0, 3, 1, 2, 4)
 
 

time: 39 us -> 38.5 us (0.987)
  waiting for transfers between devices: 8.67 us -> 5.86 us
  starting transfers between devices: 16.5 us -> 17.9 us
  other arithmetic: 0 us -> 1.33 us
  Pallas kernels: 12.6 us -> 11.9 us
    ppermute x10 -> x11, waiting for transfers between devices: 8.67 us -> 5.86 us  [across(): return lax.ppermute(value, 'atom', [(i, i ^ by) for i in range(devices)])]
    ppermute x10 -> x11, starting transfers between devices: 15.1 us -> 16.6 us  [across(): return lax.ppermute(value, 'atom', [(i, i ^ by) for i in range(devices)])]
    pallas_call x1, Pallas kernels: 5.86 us -> 4.46 us  [on_device(): call(make_form(orb), [shape((slots, height, 2 * LANES), BF)], [VM, VM], N...]
    another operation x0 -> x2, other arithmetic: none -> 1.33 us  [on_device(): spectrum = jnp.stack([shifts.astype(F32), weights])]
    pallas_call x4 -> x5, Pallas kernels: 4.58 us -> 5.1 us  [the longest x1 1.56 us: on_device(): call(make_local(mates, half), [total], [SM] + [VM] * (5 + mates), us=1.5)]
    unnamed x10 -> x6, local copies, waits for them, and re-layouts: 0.69 us -> 0.97 us
  transfers between devices with their start and end apart: 11 -> 12, of which waited for: 4 -> 3; matrix products, arithmetic and copies ran while one was open for 1% -> 1% of each run, Pallas kernels for 27% -> 22%
where the time goes in v3:
time: 38.5 us; the launch traced here: 38.3 us
  starting transfers between devices  17.9 us (46%)
  Pallas kernels  11.9 us (31%)
  waiting for transfers between devices  5.86 us (15%)
  other arithmetic  1.33 us (3%)
  local copies, waits for them, and re-layouts  1.21 us (3%)
    ppermute x11, starting transfers between devices, across(): return lax.ppermute(value, 'atom', [(i, i ^ by) for i in range(devices)])  16.6 us
    ppermute x11, waiting for transfers between devices, across(): return lax.ppermute(value, 'atom', [(i, i ^ by) for i in range(devices)])  5.86 us
    pallas_call x1, Pallas kernels, on_device(): call(make_form(orb), [shape((slots, height, 2 * LANES), BF)], [VM, VM], N...  4.46 us
    pallas_call x1, Pallas kernels, on_device(): call(make_final(mates, half, orb), [shape(x.shape, BF)], [SM] + [VM] * (2...  2.09 us
    pallas_call x1, Pallas kernels, on_device(): call(make_local(mates, half), [total], [SM] + [VM] * (5 + mates), us=1.5)  1.56 us
    another operation x2, other arithmetic, on_device(): spectrum = jnp.stack([shifts.astype(F32), weights])  1.33 us
    ppermute x1, starting transfers between devices, on_device(): lax.ppermute(after(x, low), 'energy', [(i, i - 1) for i in range(1, peers)])  1.29 us
    pallas_call x1, Pallas kernels, on_device(): call(low_kernel, [unit, shape((2 * size, atoms * span), BF), shape((2, 4...  1.24 us
  transfers between devices with their start and end apart: 12, of which 3 were waited for; matrix products, arithmetic and copies ran while one was open for 1% of the time, Pallas kernels for 22%

profile of v3, /device:TPU:0, one launch (start us, length us, event | category | flops | bytes accessed | tf_op | source)
XLA Modules:
  0.0 38.3 jit_solution(7963587426352511529)
XLA Ops:
  0.0 0.7 %convert_bitcast_fusion = f32[1,16]{1,0:T(1,128)S(1)} fusion(s32[16]{0:T(128)} %param.8), kind=kLoop, calls=%fused_computation.1 | loop fusion | flops 16 | bytes 128 | tf_op jit(solution)/shard_map/stack | solution.py:292
  0.7 0.7 %pad_maximum_fusion.spectrum = f32[2,16]{1,0:T(2,128)S(1)} fusion(f32[1,16]{1,0:T(1,128)} %bitcast.11, f32[1,16]{1,0:T(1,128)S(1)} %convert_bitcast_fusion), kind=kLoop, calls=%fused_computation | loop fusion | flops 32 | bytes 256 | tf_op jit(solution)/shard_map/stack | solution.py:292
  1.3 1.0 %copy-done = bf16[4,2,12,12,128]{4,1,3,2,0:T(2,128)(2,1)S(1)} copy-done((bf16[4,2,12,12,128]{4,1,3,2,0:T(2,128)(2,1)S(1)}, bf16[4,2,12,12,128]{4,1,3,2,0:T(2,128)(2,1)}, u32[]{:S(2)}) %copy-start) | copy-done | bytes 294936
  2.3 1.2 %shard_map.57 = (bf16[4,144,128]{2,1,0:T(8,128)(2,1)S(1)}, bf16[288,512]{1,0:T(8,128)(2,1)S(1)}, bf16[2,512,128]{2,1,0:T(8,128)(2,1)S(1)}) custom-call(f32[2,16]{1,0:T(2,128)S(1)} %pad_maximum_fusion.spectrum, bf16[1152,128]{1,0:T(8,128)(2,1)S(1)} %bitcast.9), custom_call_target="tpu_custom_call" | custom-call | flops 1200000000 | bytes 1000 | tf_op jit(solution)/shard_map/pallas_call | solution.py:294
  3.5 1.3 %collective-permute-start = (bf16[1152,128]{1,0:T(8,128)(2,1)S(1)}, bf16[1152,128]{1,0:T(8,128)(2,1)S(1)}, u32[]{:S(2)}, u32[]{:S(2)}) collective-permute-start(bf16[1152,128]{1,0:T(8,128)(2,1)S(1)} %bitcast.10), channel_id=1, source_target_pairs={{8,0},{16,8},{24,16},{9,1},{17,9},{25,17},{10,2},{18,10},{26,18},{... | collective-permute-start | bytes 884744 | tf_op jit(solution)/shard_map/ppermute | solution.py:300
  4.8 4.1 %collective-permute-start.1 = (bf16[4,144,128]{2,1,0:T(8,128)(2,1)S(1)}, bf16[4,144,128]{2,1,0:T(8,128)(2,1)S(1)}, u32[]{:S(2)}, u32[]{:S(2)}) collective-permute-start(bf16[4,144,128]{2,1,0:T(8,128)(2,1)S(1)} %get-tuple-element.20.refs_3_.refs_2_), channel_id=1, source_target_pairs={{0,4},{1,5},{2,6},{3,7},{4,0},{5,1},{6,2},{7,3},{8,12},{9,13},{10,... | collective-permute-start | bytes 442376 | tf_op jit(solution)/shard_map/ppermute | solution.py:289
  9.2 0.7 %shard_map.58.refs_4_.refs_3_ = bf16[4,144,128]{2,1,0:T(8,128)(2,1)S(1)} custom-call(bf16[288,512]{1,0:T(8,128)(2,1)S(1)} %get-tuple-element.21.apart, bf16[2,512,128]{2,1,0:T(8,128)(2,1)S(1)} %get-tuple-element.22.bands, bf16[1152,128]{1,0:T(8,128)(2,1)S(1)} %collective-permute-done.beyond), custom_call_target="tpu_custom_call" | custom-call | flops 700000000 | bytes 1000 | tf_op jit(solution)/shard_map/pallas_call | solution.py:301
  9.9 2.6 %collective-permute-start.3 = (s32[8,128]{1,0:T(8,128)S(1)}, s32[8,128]{1,0:T(8,128)S(1)}, u32[]{:S(2)}, u32[]{:S(2)}) collective-permute-start(s32[8,128]{1,0:T(8,128)S(1)} %get-tuple-element.24.refs_0_), channel_id=1, source_target_pairs={{0,3},{1,2},{2,1},{3,0},{4,7},{5,6},{6,5},{7,4},{8,11},{9,10},{10,... | collective-permute-start | bytes 12296 | tf_op jit(solution)/shard_map/ppermute | solution.py:289
  12.5 0.4 %collective-permute-start.4 = (s32[8,128]{1,0:T(8,128)S(1)}, s32[8,128]{1,0:T(8,128)S(1)}, u32[]{:S(2)}, u32[]{:S(2)}) collective-permute-start(s32[8,128]{1,0:T(8,128)S(1)} %get-tuple-element.24.refs_0_), channel_id=1, source_target_pairs={{0,2},{1,3},{2,0},{3,1},{4,6},{5,7},{6,4},{7,5},{8,10},{9,11},{10,... | collective-permute-start | bytes 12296 | tf_op jit(solution)/shard_map/ppermute | solution.py:289
  12.9 0.5 %collective-permute-start.5 = (s32[8,128]{1,0:T(8,128)S(1)}, s32[8,128]{1,0:T(8,128)S(1)}, u32[]{:S(2)}, u32[]{:S(2)}) collective-permute-start(s32[8,128]{1,0:T(8,128)S(1)} %get-tuple-element.24.refs_0_), channel_id=1, source_target_pairs={{0,1},{1,0},{2,3},{3,2},{4,5},{5,4},{6,7},{7,6},{8,9},{9,8},{10,11... | collective-permute-start | bytes 12296 | tf_op jit(solution)/shard_map/ppermute | solution.py:289
  13.4 1.9 %collective-permute-start.2 = (bf16[4,144,128]{2,1,0:T(8,128)(2,1)S(1)}, bf16[4,144,128]{2,1,0:T(8,128)(2,1)S(1)}, u32[]{:S(2)}, u32[]{:S(2)}) collective-permute-start(bf16[4,144,128]{2,1,0:T(8,128)(2,1)S(1)} %shard_map.58.refs_4_.refs_3_), channel_id=1, source_target_pairs={{0,4},{1,5},{2,6},{3,7},{4,0},{5,1},{6,2},{7,3},{8,12},{9,13},{10,... | collective-permute-start | bytes 442376 | tf_op jit(solution)/shard_map/ppermute | solution.py:289
  15.3 1.2 %collective-permute-done.1.refs_5_.refs_4_ = bf16[4,144,128]{2,1,0:T(8,128)(2,1)S(1)} collective-permute-done((bf16[4,144,128]{2,1,0:T(8,128)(2,1)S(1)}, bf16[4,144,128]{2,1,0:T(8,128)(2,1)S(1)}, u32[]{:S(2)}, u32[]{:S(2)}) %collective-permute-start.1) | collective-permute-done | bytes 147488 | tf_op jit(solution)/shard_map/ppermute | solution.py:289
  16.5 0.9 %shard_map.59 = (bf16[2,144,384]{2,1,0:T(8,128)(2,1)S(1)}, bf16[2,144,384]{2,1,0:T(8,128)(2,1)S(1)}, bf16[2,144,384]{2,1,0:T(8,128)(2,1)S(1)}) custom-call(s32[8,128]{1,0:T(8,128)S(1)} %collective-permute-done.3.refs_0_, s32[8,128]{1,0:T(8,128)S(1)} %collective-permute-done.4.refs_1_, s32[8,128]{1,0:T(8,128)S(1)} %collective-permute-done.5.refs_2_, ...), custom_call_target="tpu_custom_call" | custom-call | flops 1000000000 | bytes 1000 | tf_op jit(solution)/shard_map/pallas_call | solution.py:308
  17.4 2.3 %collective-permute-start.6 = (bf16[2,144,384]{2,1,0:T(8,128)(2,1)S(1)}, bf16[2,144,384]{2,1,0:T(8,128)(2,1)S(1)}, u32[]{:S(2)}, u32[]{:S(2)}) collective-permute-start(bf16[2,144,384]{2,1,0:T(8,128)(2,1)S(1)} %get-tuple-element.25), channel_id=1, source_target_pairs={{0,3},{1,2},{2,1},{3,0},{4,7},{5,6},{6,5},{7,4},{8,11},{9,10},{10,... | collective-permute-start | bytes 663560 | tf_op jit(solution)/shard_map/ppermute | solution.py:289
  19.7 1.2 %collective-permute-start.7 = (bf16[2,144,384]{2,1,0:T(8,128)(2,1)S(1)}, bf16[2,144,384]{2,1,0:T(8,128)(2,1)S(1)}, u32[]{:S(2)}, u32[]{:S(2)}) collective-permute-start(bf16[2,144,384]{2,1,0:T(8,128)(2,1)S(1)} %get-tuple-element.26), channel_id=1, source_target_pairs={{0,2},{1,3},{2,0},{3,1},{4,6},{5,7},{6,4},{7,5},{8,10},{9,11},{10,... | collective-permute-start | bytes 663560 | tf_op jit(solution)/shard_map/ppermute | solution.py:289
  21.0 0.2 reshape.9.x
  21.2 4.5 %shard_map.56.refs_1_ = bf16[32,192,256]{2,1,0:T(8,128)(2,1)S(1)} custom-call(s32[4,24]{1,0:T(4,128)S(1)} %get-tuple-element.19.target, bf16[288,144]{1,0:T(8,128)(2,1)S(1)} %reshape.9.x), custom_call_target="tpu_custom_call" | custom-call | flops 10000000 | bytes 1000 | tf_op jit(solution)/shard_map/pallas_call | solution.py:316
  25.7 0.8 %shard_map.61 = (bf16[2,144,128]{2,1,0:T(8,128)(2,1)S(1)}, bf16[2,144,128]{2,1,0:T(8,128)(2,1)S(1)}, bf16[2,144,128]{2,1,0:T(8,128)(2,1)S(1)}) custom-call(s32[8,128]{1,0:T(8,128)S(1)} %collective-permute-done.3.refs_0_, s32[8,128]{1,0:T(8,128)S(1)} %collective-permute-done.4.refs_1_, s32[8,128]{1,0:T(8,128)S(1)} %collective-permute-done.5.refs_2_, ...), custom_call_target="tpu_custom_call" | custom-call | flops 1000000000 | bytes 1000 | tf_op jit(solution)/shard_map/pallas_call | solution.py:310
  26.5 2.3 %collective-permute-start.9 = (bf16[2,144,128]{2,1,0:T(8,128)(2,1)S(1)}, bf16[2,144,128]{2,1,0:T(8,128)(2,1)S(1)}, u32[]{:S(2)}, u32[]{:S(2)}) collective-permute-start(bf16[2,144,128]{2,1,0:T(8,128)(2,1)S(1)} %get-tuple-element.28), channel_id=1, source_target_pairs={{0,3},{1,2},{2,1},{3,0},{4,7},{5,6},{6,5},{7,4},{8,11},{9,10},{10,... | collective-permute-start | bytes 221192 | tf_op jit(solution)/shard_map/ppermute | solution.py:289
  28.8 1.2 %collective-permute-start.10 = (bf16[2,144,128]{2,1,0:T(8,128)(2,1)S(1)}, bf16[2,144,128]{2,1,0:T(8,128)(2,1)S(1)}, u32[]{:S(2)}, u32[]{:S(2)}) collective-permute-start(bf16[2,144,128]{2,1,0:T(8,128)(2,1)S(1)} %get-tuple-element.29), channel_id=1, source_target_pairs={{0,2},{1,3},{2,0},{3,1},{4,6},{5,7},{6,4},{7,5},{8,10},{9,11},{10,... | collective-permute-start | bytes 221192 | tf_op jit(solution)/shard_map/ppermute | solution.py:289
  30.0 3.0 %collective-permute-done.7.refs_7_.refs_4_ = bf16[2,144,384]{2,1,0:T(8,128)(2,1)S(1)} collective-permute-done((bf16[2,144,384]{2,1,0:T(8,128)(2,1)S(1)}, bf16[2,144,384]{2,1,0:T(8,128)(2,1)S(1)}, u32[]{:S(2)}, u32[]{:S(2)}) %collective-permute-start.7) | collective-permute-done | bytes 221216 | tf_op jit(solution)/shard_map/ppermute | solution.py:289
  33.1 1.6 %shard_map.60.refs_2_ = f32[4,192,256]{2,1,0:T(8,128)S(1)} custom-call(s32[8,128]{1,0:T(8,128)S(1)} %get-tuple-element.24.refs_0_, bf16[32,192,256]{2,1,0:T(8,128)(2,1)S(1)} %shard_map.56.refs_1_, bf16[4,144,128]{2,1,0:T(8,128)(2,1)S(1)} %get-tuple-element.20.refs_3_.refs_2_, bf16[4,144,128]{2,1,0:T(8,128)(2,1)S(1)} %shard_map.58.refs_4_.refs_3_, ...), custom_call_target="tpu_custom_call" | custom-call | flops 1500000000 | bytes 1000 | tf_op jit(solution)/shard_map/pallas_call | solution.py:330
  34.6 1.6 %collective-permute-done.10.refs_7_ = bf16[2,144,128]{2,1,0:T(8,128)(2,1)S(1)} collective-permute-done((bf16[2,144,128]{2,1,0:T(8,128)(2,1)S(1)}, bf16[2,144,128]{2,1,0:T(8,128)(2,1)S(1)}, u32[]{:S(2)}, u32[]{:S(2)}) %collective-permute-start.10) | collective-permute-done | bytes 73760 | tf_op jit(solution)/shard_map/ppermute | solution.py:289
  36.2 2.1 %shard_map.62 = bf16[1152,128]{1,0:T(8,128)(2,1)} custom-call(s32[8,128]{1,0:T(8,128)S(1)} %get-tuple-element.24.refs_0_, bf16[32,192,256]{2,1,0:T(8,128)(2,1)S(1)} %shard_map.56.refs_1_, f32[4,192,256]{2,1,0:T(8,128)S(1)} %shard_map.60.refs_2_, bf16[2,144,384]{2,1,0:T(8,128)(2,1)S(1)} %collective-permute-done.6.refs_6_.refs_3_, ...), custom_call_target="tpu_custom_call" | custom-call | flops 1000000000 | bytes 1000 | tf_op jit(solution)/shard_map/pallas_call | solution.py:333
  (17 shorter events, 0.3 us)
Async XLA Ops:
  0.0 8.9 %copy-start.1 = (s32[4,24]{1,0:T(4,128)S(1)}, s32[4,24]{1,0:T(4,128)}, u32[]{:S(2)}) copy-start(s32[4,24]{1,0:T(4,128)} %names.1) | copy-start | bytes 1156
  1.3 1.0 %copy-start = (bf16[4,2,12,12,128]{4,1,3,2,0:T(2,128)(2,1)S(1)}, bf16[4,2,12,12,128]{4,1,3,2,0:T(2,128)(2,1)}, u32[]{:S(2)}) copy-start(bf16[4,2,12,12,128]{4,1,3,2,0:T(2,128)(2,1)} %param.5) | copy-start | bytes 884740
  3.5 5.6 %collective-permute-start = (bf16[1152,128]{1,0:T(8,128)(2,1)S(1)}, bf16[1152,128]{1,0:T(8,128)(2,1)S(1)}, u32[]{:S(2)}, u32[]{:S(2)}) collective-permute-start(bf16[1152,128]{1,0:T(8,128)(2,1)S(1)} %bitcast.10), channel_id=1, source_target_pairs={{8,0},{16,8},{24,16},{9,1},{17,9},{25,17},{10,2},{18,10},{26,18},{... | collective-permute-start | bytes 884744 | tf_op jit(solution)/shard_map/ppermute | solution.py:300
  4.8 11.7 %collective-permute-start.1 = (bf16[4,144,128]{2,1,0:T(8,128)(2,1)S(1)}, bf16[4,144,128]{2,1,0:T(8,128)(2,1)S(1)}, u32[]{:S(2)}, u32[]{:S(2)}) collective-permute-start(bf16[4,144,128]{2,1,0:T(8,128)(2,1)S(1)} %get-tuple-element.20.refs_3_.refs_2_), channel_id=1, source_target_pairs={{0,4},{1,5},{2,6},{3,7},{4,0},{5,1},{6,2},{7,3},{8,12},{9,13},{10,... | collective-permute-start | bytes 442376 | tf_op jit(solution)/shard_map/ppermute | solution.py:289
  9.2 11.8 %copy-start.2 = (bf16[4,10368]{1,0:T(4,128)(2,1)S(1)}, bf16[4,10368]{1,0:T(4,128)(2,1)}, u32[]{:S(2)}) copy-start(bf16[4,10368]{1,0:T(4,128)(2,1)} %param.6) | copy-start | bytes 248836
  9.9 6.6 %collective-permute-start.3 = (s32[8,128]{1,0:T(8,128)S(1)}, s32[8,128]{1,0:T(8,128)S(1)}, u32[]{:S(2)}, u32[]{:S(2)}) collective-permute-start(s32[8,128]{1,0:T(8,128)S(1)} %get-tuple-element.24.refs_0_), channel_id=1, source_target_pairs={{0,3},{1,2},{2,1},{3,0},{4,7},{5,6},{6,5},{7,4},{8,11},{9,10},{10,... | collective-permute-start | bytes 12296 | tf_op jit(solution)/shard_map/ppermute | solution.py:289
  12.5 4.0 %collective-permute-start.4 = (s32[8,128]{1,0:T(8,128)S(1)}, s32[8,128]{1,0:T(8,128)S(1)}, u32[]{:S(2)}, u32[]{:S(2)}) collective-permute-start(s32[8,128]{1,0:T(8,128)S(1)} %get-tuple-element.24.refs_0_), channel_id=1, source_target_pairs={{0,2},{1,3},{2,0},{3,1},{4,6},{5,7},{6,4},{7,5},{8,10},{9,11},{10,... | collective-permute-start | bytes 12296 | tf_op jit(solution)/shard_map/ppermute | solution.py:289
  12.9 3.6 %collective-permute-start.5 = (s32[8,128]{1,0:T(8,128)S(1)}, s32[8,128]{1,0:T(8,128)S(1)}, u32[]{:S(2)}, u32[]{:S(2)}) collective-permute-start(s32[8,128]{1,0:T(8,128)S(1)} %get-tuple-element.24.refs_0_), channel_id=1, source_target_pairs={{0,1},{1,0},{2,3},{3,2},{4,5},{5,4},{6,7},{7,6},{8,9},{9,8},{10,11... | collective-permute-start | bytes 12296 | tf_op jit(solution)/shard_map/ppermute | solution.py:289
  13.4 12.2 %collective-permute-start.2 = (bf16[4,144,128]{2,1,0:T(8,128)(2,1)S(1)}, bf16[4,144,128]{2,1,0:T(8,128)(2,1)S(1)}, u32[]{:S(2)}, u32[]{:S(2)}) collective-permute-start(bf16[4,144,128]{2,1,0:T(8,128)(2,1)S(1)} %shard_map.58.refs_4_.refs_3_), channel_id=1, source_target_pairs={{0,4},{1,5},{2,6},{3,7},{4,0},{5,1},{6,2},{7,3},{8,12},{9,13},{10,... | collective-permute-start | bytes 442376 | tf_op jit(solution)/shard_map/ppermute | solution.py:289
  17.4 12.6 %collective-permute-start.6 = (bf16[2,144,384]{2,1,0:T(8,128)(2,1)S(1)}, bf16[2,144,384]{2,1,0:T(8,128)(2,1)S(1)}, u32[]{:S(2)}, u32[]{:S(2)}) collective-permute-start(bf16[2,144,384]{2,1,0:T(8,128)(2,1)S(1)} %get-tuple-element.25), channel_id=1, source_target_pairs={{0,3},{1,2},{2,1},{3,0},{4,7},{5,6},{6,5},{7,4},{8,11},{9,10},{10,... | collective-permute-start | bytes 663560 | tf_op jit(solution)/shard_map/ppermute | solution.py:289
  19.7 13.3 %collective-permute-start.7 = (bf16[2,144,384]{2,1,0:T(8,128)(2,1)S(1)}, bf16[2,144,384]{2,1,0:T(8,128)(2,1)S(1)}, u32[]{:S(2)}, u32[]{:S(2)}) collective-permute-start(bf16[2,144,384]{2,1,0:T(8,128)(2,1)S(1)} %get-tuple-element.26), channel_id=1, source_target_pairs={{0,2},{1,3},{2,0},{3,1},{4,6},{5,7},{6,4},{7,5},{8,10},{9,11},{10,... | collective-permute-start | bytes 663560 | tf_op jit(solution)/shard_map/ppermute | solution.py:289
  20.9 12.1 %collective-permute-start.8 = (bf16[2,144,384]{2,1,0:T(8,128)(2,1)S(1)}, bf16[2,144,384]{2,1,0:T(8,128)(2,1)S(1)}, u32[]{:S(2)}, u32[]{:S(2)}) collective-permute-start(bf16[2,144,384]{2,1,0:T(8,128)(2,1)S(1)} %get-tuple-element.27), channel_id=1, source_target_pairs={{0,1},{1,0},{2,3},{3,2},{4,5},{5,4},{6,7},{7,6},{8,9},{9,8},{10,11... | collective-permute-start | bytes 663560 | tf_op jit(solution)/shard_map/ppermute | solution.py:289
  26.5 8.2 %collective-permute-start.9 = (bf16[2,144,128]{2,1,0:T(8,128)(2,1)S(1)}, bf16[2,144,128]{2,1,0:T(8,128)(2,1)S(1)}, u32[]{:S(2)}, u32[]{:S(2)}) collective-permute-start(bf16[2,144,128]{2,1,0:T(8,128)(2,1)S(1)} %get-tuple-element.28), channel_id=1, source_target_pairs={{0,3},{1,2},{2,1},{3,0},{4,7},{5,6},{6,5},{7,4},{8,11},{9,10},{10,... | collective-permute-start | bytes 221192 | tf_op jit(solution)/shard_map/ppermute | solution.py:289
  28.8 7.5 %collective-permute-start.10 = (bf16[2,144,128]{2,1,0:T(8,128)(2,1)S(1)}, bf16[2,144,128]{2,1,0:T(8,128)(2,1)S(1)}, u32[]{:S(2)}, u32[]{:S(2)}) collective-permute-start(bf16[2,144,128]{2,1,0:T(8,128)(2,1)S(1)} %get-tuple-element.29), channel_id=1, source_target_pairs={{0,2},{1,3},{2,0},{3,1},{4,6},{5,7},{6,4},{7,5},{8,10},{9,11},{10,... | collective-permute-start | bytes 221192 | tf_op jit(solution)/shard_map/ppermute | solution.py:289
  30.0 6.2 %collective-permute-start.11 = (bf16[2,144,128]{2,1,0:T(8,128)(2,1)S(1)}, bf16[2,144,128]{2,1,0:T(8,128)(2,1)S(1)}, u32[]{:S(2)}, u32[]{:S(2)}) collective-permute-start(bf16[2,144,128]{2,1,0:T(8,128)(2,1)S(1)} %get-tuple-element.30), channel_id=1, source_target_pairs={{0,1},{1,0},{2,3},{3,2},{4,5},{5,4},{6,7},{7,6},{8,9},{9,8},{10,11... | collective-permute-start | bytes 221192 | tf_op jit(solution)/shard_map/ppermute | solution.py:289

commit v4 on v3

--- a/solution.py
+++ b/solution.py
@@ -55,15 +55,15 @@
     return jnp.concatenate(rows, axis=0)
 
 
-def low_kernel(spectrum, x, out, apart, bands):
+def low_kernel(shifts, weights, x, out, apart, bands):
     atoms, size, span = out.shape
     half = span // 2
     lane = iota((2 * span, span), 1)
     first = lane < half
-    gap = (iota((2 * span, span), 0) - half - jnp.where(first, lane, lane - half)).astype(F32)
+    gap = iota((2 * span, span), 0) - half - jnp.where(first, lane, lane - half)
     band = jnp.zeros(gap.shape, F32)
-    for q in range(spectrum.shape[1]):
-        band = band + jnp.where(gap == spectrum[0, q], spectrum[1, q], 0.0)
+    for q in range(shifts.shape[0]):
+        band = band + jnp.where(gap == shifts[q], weights[q], 0.0)
     rounded = band.astype(BF).astype(F32)
 
     def parted(part, mask):
@@ -289,14 +289,13 @@
         return lax.ppermute(value, "atom", [(i, i ^ by) for i in range(devices)])
 
     x = green.transpose(0, 2, 3, 1, 4).reshape(atoms * size * 2, span)
-    spectrum = jnp.stack([shifts.astype(F32), weights])
     unit = shape((atoms, size, span), BF)
     low, apart, bands = call(
         low_kernel,
         [unit, shape((2 * size, atoms * span), BF), shape((2, 4 * span, span), BF)],
-        [SM, VM],
-        us=1.2,
-    )(spectrum, x)
+        [SM, SM, VM],
+        us=0.01,
+    )(shifts, weights, x)
     beyond = lax.ppermute(after(x, low), "energy", [(i, i - 1) for i in range(1, peers)])
     (high,) = call(high_kernel, [unit], [VM] * 3, us=0.7)(apart, bands, beyond)
     mirror = across(low, half), across(high, half)

time: 38.5 us -> 38.4 us (level)
  other arithmetic: 1.33 us -> 0 us
  local copies, waits for them, and re-layouts: 1.21 us -> 2.24 us
  Pallas kernels: 11.9 us -> 12.3 us
  starting transfers between devices: 17.9 us -> 17.5 us
    another operation x2 -> x0, other arithmetic: 1.33 us -> none  [on_device(): spectrum = jnp.stack([shifts.astype(F32), weights])]
    unnamed x6 -> x8, local copies, waits for them, and re-layouts: 0.97 us -> 2 us
    ppermute x11, starting transfers between devices: 16.6 us -> 16.2 us  [across(): return lax.ppermute(value, 'atom', [(i, i ^ by) for i in range(devices)])]
    pallas_call x1, Pallas kernels: 1.24 us -> 1.65 us  [on_device(): call(low_kernel, [unit, shape((2 * size, atoms * span), BF), shape((2, 4...]
  transfers between devices with their start and end apart: 12 -> 12, of which waited for: 3 -> 5; matrix products, arithmetic and copies ran while one was open for 1% -> 1% of each run, Pallas kernels for 22% -> 22%
where the time goes in v4:
time: 38.4 us; the launch traced here: 38.2 us
  starting transfers between devices  17.5 us (46%)
  Pallas kernels  12.3 us (32%)
  waiting for transfers between devices  6.15 us (16%)
  local copies, waits for them, and re-layouts  2.24 us (6%)
    ppermute x11, starting transfers between devices, across(): return lax.ppermute(value, 'atom', [(i, i ^ by) for i in range(devices)])  16.2 us
    ppermute x11, waiting for transfers between devices, across(): return lax.ppermute(value, 'atom', [(i, i ^ by) for i in range(devices)])  6.15 us
    pallas_call x1, Pallas kernels, on_device(): call(make_form(orb), [shape((slots, height, 2 * LANES), BF)], [VM, VM], N...  4.46 us
    pallas_call x1, Pallas kernels, on_device(): call(make_final(mates, half, orb), [shape(x.shape, BF)], [SM] + [VM] * (2...  2.09 us
    unnamed x8, local copies, waits for them, and re-layouts  2 us
    pallas_call x1, Pallas kernels, on_device(): call(low_kernel, [unit, shape((2 * size, atoms * span), BF), shape((2, 4...  1.65 us
    pallas_call x1, Pallas kernels, on_device(): call(make_local(mates, half), [total], [SM] + [VM] * (5 + mates), us=1.5)  1.56 us
    ppermute x1, starting transfers between devices, on_device(): lax.ppermute(after(x, low), 'energy', [(i, i - 1) for i in range(1, peers)])  1.29 us
  transfers between devices with their start and end apart: 12, of which 5 were waited for; matrix products, arithmetic and copies ran while one was open for 1% of the time, Pallas kernels for 22%

profile of v4, /device:TPU:0, one launch (start us, length us, event | category | flops | bytes accessed | tf_op | source)
XLA Modules:
  0.0 38.2 jit_solution(6603715492517515184)
XLA Ops:
  0.0 0.7 %copy-done = s32[16]{0:T(128)S(1)} copy-done((s32[16]{0:T(128)S(1)}, s32[16]{0:T(128)}, u32[]{:S(2)}) %copy-start) | copy-done | bytes 88
  0.7 0.7 %copy-done.1 = f32[16]{0:T(128)S(1)} copy-done((f32[16]{0:T(128)S(1)}, f32[16]{0:T(128)}, u32[]{:S(2)}) %copy-start.1) | copy-done | bytes 88
  1.3 1.7 %shard_map.57 = (bf16[4,144,128]{2,1,0:T(8,128)(2,1)S(1)}, bf16[288,512]{1,0:T(8,128)(2,1)S(1)}, bf16[2,512,128]{2,1,0:T(8,128)(2,1)S(1)}) custom-call(s32[16]{0:T(128)S(1)} %copy-done, f32[16]{0:T(128)S(1)} %copy-done.1, bf16[1152,128]{1,0:T(8,128)(2,1)} %bitcast.1.x), custom_call_target="tpu_custom_call" | custom-call | flops 10000000 | bytes 1000 | tf_op jit(solution)/shard_map/pallas_call | solution.py:293
  3.0 1.3 %collective-permute-start = (bf16[1152,128]{1,0:T(8,128)(2,1)}, bf16[1152,128]{1,0:T(8,128)(2,1)S(1)}, u32[]{:S(2)}, u32[]{:S(2)}) collective-permute-start(bf16[1152,128]{1,0:T(8,128)(2,1)} %bitcast.1.x), channel_id=1, source_target_pairs={{8,0},{16,8},{24,16},{9,1},{17,9},{25,17},{10,2},{18,10},{26,18},{... | collective-permute-start | bytes 884744 | tf_op jit(solution)/shard_map/ppermute | solution.py:299
  4.3 4.1 %collective-permute-start.1 = (bf16[4,144,128]{2,1,0:T(8,128)(2,1)S(1)}, bf16[4,144,128]{2,1,0:T(8,128)(2,1)S(1)}, u32[]{:S(2)}, u32[]{:S(2)}) collective-permute-start(bf16[4,144,128]{2,1,0:T(8,128)(2,1)S(1)} %get-tuple-element.20.refs_3_.refs_2_), channel_id=1, source_target_pairs={{0,4},{1,5},{2,6},{3,7},{4,0},{5,1},{6,2},{7,3},{8,12},{9,13},{10,... | collective-permute-start | bytes 442376 | tf_op jit(solution)/shard_map/ppermute | solution.py:289
  8.4 0.7 %copy-done.2 = s32[4,24]{1,0:T(4,128)S(1)} copy-done((s32[4,24]{1,0:T(4,128)S(1)}, s32[4,24]{1,0:T(4,128)}, u32[]{:S(2)}) %copy-start.2) | copy-done | bytes 408
  9.3 0.7 %shard_map.58.refs_4_.refs_3_ = bf16[4,144,128]{2,1,0:T(8,128)(2,1)S(1)} custom-call(bf16[288,512]{1,0:T(8,128)(2,1)S(1)} %get-tuple-element.21.apart, bf16[2,512,128]{2,1,0:T(8,128)(2,1)S(1)} %get-tuple-element.22.bands, bf16[1152,128]{1,0:T(8,128)(2,1)S(1)} %collective-permute-done.beyond), custom_call_target="tpu_custom_call" | custom-call | flops 700000000 | bytes 1000 | tf_op jit(solution)/shard_map/pallas_call | solution.py:300
  10.0 2.6 %collective-permute-start.3 = (s32[8,128]{1,0:T(8,128)S(1)}, s32[8,128]{1,0:T(8,128)S(1)}, u32[]{:S(2)}, u32[]{:S(2)}) collective-permute-start(s32[8,128]{1,0:T(8,128)S(1)} %get-tuple-element.24.refs_0_), channel_id=1, source_target_pairs={{0,3},{1,2},{2,1},{3,0},{4,7},{5,6},{6,5},{7,4},{8,11},{9,10},{10,... | collective-permute-start | bytes 12296 | tf_op jit(solution)/shard_map/ppermute | solution.py:289
  13.0 0.5 %collective-permute-start.5 = (s32[8,128]{1,0:T(8,128)S(1)}, s32[8,128]{1,0:T(8,128)S(1)}, u32[]{:S(2)}, u32[]{:S(2)}) collective-permute-start(s32[8,128]{1,0:T(8,128)S(1)} %get-tuple-element.24.refs_0_), channel_id=1, source_target_pairs={{0,1},{1,0},{2,3},{3,2},{4,5},{5,4},{6,7},{7,6},{8,9},{9,8},{10,11... | collective-permute-start | bytes 12296 | tf_op jit(solution)/shard_map/ppermute | solution.py:289
  13.5 1.4 %collective-permute-start.2 = (bf16[4,144,128]{2,1,0:T(8,128)(2,1)S(1)}, bf16[4,144,128]{2,1,0:T(8,128)(2,1)S(1)}, u32[]{:S(2)}, u32[]{:S(2)}) collective-permute-start(bf16[4,144,128]{2,1,0:T(8,128)(2,1)S(1)} %shard_map.58.refs_4_.refs_3_), channel_id=1, source_target_pairs={{0,4},{1,5},{2,6},{3,7},{4,0},{5,1},{6,2},{7,3},{8,12},{9,13},{10,... | collective-permute-start | bytes 442376 | tf_op jit(solution)/shard_map/ppermute | solution.py:289
  14.9 1.0 %collective-permute-done.1.refs_5_.refs_4_ = bf16[4,144,128]{2,1,0:T(8,128)(2,1)S(1)} collective-permute-done((bf16[4,144,128]{2,1,0:T(8,128)(2,1)S(1)}, bf16[4,144,128]{2,1,0:T(8,128)(2,1)S(1)}, u32[]{:S(2)}, u32[]{:S(2)}) %collective-permute-start.1) | collective-permute-done | bytes 147488 | tf_op jit(solution)/shard_map/ppermute | solution.py:289
  16.6 0.9 %shard_map.59 = (bf16[2,144,384]{2,1,0:T(8,128)(2,1)S(1)}, bf16[2,144,384]{2,1,0:T(8,128)(2,1)S(1)}, bf16[2,144,384]{2,1,0:T(8,128)(2,1)S(1)}) custom-call(s32[8,128]{1,0:T(8,128)S(1)} %collective-permute-done.3.refs_0_, s32[8,128]{1,0:T(8,128)S(1)} %collective-permute-done.4.refs_1_, s32[8,128]{1,0:T(8,128)S(1)} %collective-permute-done.5.refs_2_, ...), custom_call_target="tpu_custom_call" | custom-call | flops 1000000000 | bytes 1000 | tf_op jit(solution)/shard_map/pallas_call | solution.py:307
  17.5 1.6 %collective-permute-start.6 = (bf16[2,144,384]{2,1,0:T(8,128)(2,1)S(1)}, bf16[2,144,384]{2,1,0:T(8,128)(2,1)S(1)}, u32[]{:S(2)}, u32[]{:S(2)}) collective-permute-start(bf16[2,144,384]{2,1,0:T(8,128)(2,1)S(1)} %get-tuple-element.25), channel_id=1, source_target_pairs={{0,3},{1,2},{2,1},{3,0},{4,7},{5,6},{6,5},{7,4},{8,11},{9,10},{10,... | collective-permute-start | bytes 663560 | tf_op jit(solution)/shard_map/ppermute | solution.py:289
  19.1 1.3 %collective-permute-start.7 = (bf16[2,144,384]{2,1,0:T(8,128)(2,1)S(1)}, bf16[2,144,384]{2,1,0:T(8,128)(2,1)S(1)}, u32[]{:S(2)}, u32[]{:S(2)}) collective-permute-start(bf16[2,144,384]{2,1,0:T(8,128)(2,1)S(1)} %get-tuple-element.26), channel_id=1, source_target_pairs={{0,2},{1,3},{2,0},{3,1},{4,6},{5,7},{6,4},{7,5},{8,10},{9,11},{10,... | collective-permute-start | bytes 663560 | tf_op jit(solution)/shard_map/ppermute | solution.py:289
  20.4 0.6 %collective-permute-start.8 = (bf16[2,144,384]{2,1,0:T(8,128)(2,1)S(1)}, bf16[2,144,384]{2,1,0:T(8,128)(2,1)S(1)}, u32[]{:S(2)}, u32[]{:S(2)}) collective-permute-start(bf16[2,144,384]{2,1,0:T(8,128)(2,1)S(1)} %get-tuple-element.27), channel_id=1, source_target_pairs={{0,1},{1,0},{2,3},{3,2},{4,5},{5,4},{6,7},{7,6},{8,9},{9,8},{10,11... | collective-permute-start | bytes 663560 | tf_op jit(solution)/shard_map/ppermute | solution.py:289
  21.3 4.5 %shard_map.56.refs_1_ = bf16[32,192,256]{2,1,0:T(8,128)(2,1)S(1)} custom-call(s32[4,24]{1,0:T(4,128)S(1)} %get-tuple-element.19.target, bf16[288,144]{1,0:T(8,128)(2,1)S(1)} %reshape.9.x), custom_call_target="tpu_custom_call" | custom-call | flops 10000000 | bytes 1000 | tf_op jit(solution)/shard_map/pallas_call | solution.py:315
  25.8 0.8 %shard_map.61 = (bf16[2,144,128]{2,1,0:T(8,128)(2,1)S(1)}, bf16[2,144,128]{2,1,0:T(8,128)(2,1)S(1)}, bf16[2,144,128]{2,1,0:T(8,128)(2,1)S(1)}) custom-call(s32[8,128]{1,0:T(8,128)S(1)} %collective-permute-done.3.refs_0_, s32[8,128]{1,0:T(8,128)S(1)} %collective-permute-done.4.refs_1_, s32[8,128]{1,0:T(8,128)S(1)} %collective-permute-done.5.refs_2_, ...), custom_call_target="tpu_custom_call" | custom-call | flops 1000000000 | bytes 1000 | tf_op jit(solution)/shard_map/pallas_call | solution.py:309
  26.6 1.6 %collective-permute-start.9 = (bf16[2,144,128]{2,1,0:T(8,128)(2,1)S(1)}, bf16[2,144,128]{2,1,0:T(8,128)(2,1)S(1)}, u32[]{:S(2)}, u32[]{:S(2)}) collective-permute-start(bf16[2,144,128]{2,1,0:T(8,128)(2,1)S(1)} %get-tuple-element.28), channel_id=1, source_target_pairs={{0,3},{1,2},{2,1},{3,0},{4,7},{5,6},{6,5},{7,4},{8,11},{9,10},{10,... | collective-permute-start | bytes 221192 | tf_op jit(solution)/shard_map/ppermute | solution.py:289
  28.2 1.3 %collective-permute-start.10 = (bf16[2,144,128]{2,1,0:T(8,128)(2,1)S(1)}, bf16[2,144,128]{2,1,0:T(8,128)(2,1)S(1)}, u32[]{:S(2)}, u32[]{:S(2)}) collective-permute-start(bf16[2,144,128]{2,1,0:T(8,128)(2,1)S(1)} %get-tuple-element.29), channel_id=1, source_target_pairs={{0,2},{1,3},{2,0},{3,1},{4,6},{5,7},{6,4},{7,5},{8,10},{9,11},{10,... | collective-permute-start | bytes 221192 | tf_op jit(solution)/shard_map/ppermute | solution.py:289
  29.5 0.6 %collective-permute-start.11 = (bf16[2,144,128]{2,1,0:T(8,128)(2,1)S(1)}, bf16[2,144,128]{2,1,0:T(8,128)(2,1)S(1)}, u32[]{:S(2)}, u32[]{:S(2)}) collective-permute-start(bf16[2,144,128]{2,1,0:T(8,128)(2,1)S(1)} %get-tuple-element.30), channel_id=1, source_target_pairs={{0,1},{1,0},{2,3},{3,2},{4,5},{5,4},{6,7},{7,6},{8,9},{9,8},{10,11... | collective-permute-start | bytes 221192 | tf_op jit(solution)/shard_map/ppermute | solution.py:289
  30.1 2.9 %collective-permute-done.7.refs_7_.refs_4_ = bf16[2,144,384]{2,1,0:T(8,128)(2,1)S(1)} collective-permute-done((bf16[2,144,384]{2,1,0:T(8,128)(2,1)S(1)}, bf16[2,144,384]{2,1,0:T(8,128)(2,1)S(1)}, u32[]{:S(2)}, u32[]{:S(2)}) %collective-permute-start.7) | collective-permute-done | bytes 221216 | tf_op jit(solution)/shard_map/ppermute | solution.py:289
  33.0 1.6 %shard_map.60.refs_2_ = f32[4,192,256]{2,1,0:T(8,128)S(1)} custom-call(s32[8,128]{1,0:T(8,128)S(1)} %get-tuple-element.24.refs_0_, bf16[32,192,256]{2,1,0:T(8,128)(2,1)S(1)} %shard_map.56.refs_1_, bf16[4,144,128]{2,1,0:T(8,128)(2,1)S(1)} %get-tuple-element.20.refs_3_.refs_2_, bf16[4,144,128]{2,1,0:T(8,128)(2,1)S(1)} %shard_map.58.refs_4_.refs_3_, ...), custom_call_target="tpu_custom_call" | custom-call | flops 1500000000 | bytes 1000 | tf_op jit(solution)/shard_map/pallas_call | solution.py:329
  34.6 1.6 %collective-permute-done.10.refs_7_ = bf16[2,144,128]{2,1,0:T(8,128)(2,1)S(1)} collective-permute-done((bf16[2,144,128]{2,1,0:T(8,128)(2,1)S(1)}, bf16[2,144,128]{2,1,0:T(8,128)(2,1)S(1)}, u32[]{:S(2)}, u32[]{:S(2)}) %collective-permute-start.10) | collective-permute-done | bytes 73760 | tf_op jit(solution)/shard_map/ppermute | solution.py:289
  36.1 2.1 %shard_map.62 = bf16[1152,128]{1,0:T(8,128)(2,1)} custom-call(s32[8,128]{1,0:T(8,128)S(1)} %get-tuple-element.24.refs_0_, bf16[32,192,256]{2,1,0:T(8,128)(2,1)S(1)} %shard_map.56.refs_1_, f32[4,192,256]{2,1,0:T(8,128)S(1)} %shard_map.60.refs_2_, bf16[2,144,384]{2,1,0:T(8,128)(2,1)S(1)} %collective-permute-done.6.refs_6_.refs_3_, ...), custom_call_target="tpu_custom_call" | custom-call | flops 1000000000 | bytes 1000 | tf_op jit(solution)/shard_map/pallas_call | solution.py:332
  (17 shorter events, 1.6 us)
Async XLA Ops:
  0.0 0.7 %copy-start = (s32[16]{0:T(128)S(1)}, s32[16]{0:T(128)}, u32[]{:S(2)}) copy-start(s32[16]{0:T(128)} %shifts.1) | copy-start | bytes 196
  0.7 0.7 %copy-start.1 = (f32[16]{0:T(128)S(1)}, f32[16]{0:T(128)}, u32[]{:S(2)}) copy-start(f32[16]{0:T(128)} %weights.1) | copy-start | bytes 196
  3.0 6.3 %collective-permute-start = (bf16[1152,128]{1,0:T(8,128)(2,1)}, bf16[1152,128]{1,0:T(8,128)(2,1)S(1)}, u32[]{:S(2)}, u32[]{:S(2)}) collective-permute-start(bf16[1152,128]{1,0:T(8,128)(2,1)} %bitcast.1.x), channel_id=1, source_target_pairs={{8,0},{16,8},{24,16},{9,1},{17,9},{25,17},{10,2},{18,10},{26,18},{... | collective-permute-start | bytes 884744 | tf_op jit(solution)/shard_map/ppermute | solution.py:299
  4.3 11.7 %collective-permute-start.1 = (bf16[4,144,128]{2,1,0:T(8,128)(2,1)S(1)}, bf16[4,144,128]{2,1,0:T(8,128)(2,1)S(1)}, u32[]{:S(2)}, u32[]{:S(2)}) collective-permute-start(bf16[4,144,128]{2,1,0:T(8,128)(2,1)S(1)} %get-tuple-element.20.refs_3_.refs_2_), channel_id=1, source_target_pairs={{0,4},{1,5},{2,6},{3,7},{4,0},{5,1},{6,2},{7,3},{8,12},{9,13},{10,... | collective-permute-start | bytes 442376 | tf_op jit(solution)/shard_map/ppermute | solution.py:289
  8.4 0.7 %copy-start.2 = (s32[4,24]{1,0:T(4,128)S(1)}, s32[4,24]{1,0:T(4,128)}, u32[]{:S(2)}) copy-start(s32[4,24]{1,0:T(4,128)} %names.1) | copy-start | bytes 1156
  9.3 11.8 %copy-start.3 = (bf16[4,10368]{1,0:T(4,128)(2,1)S(1)}, bf16[4,10368]{1,0:T(4,128)(2,1)}, u32[]{:S(2)}) copy-start(bf16[4,10368]{1,0:T(4,128)(2,1)} %param.6) | copy-start | bytes 248836
  10.0 5.9 %collective-permute-start.3 = (s32[8,128]{1,0:T(8,128)S(1)}, s32[8,128]{1,0:T(8,128)S(1)}, u32[]{:S(2)}, u32[]{:S(2)}) collective-permute-start(s32[8,128]{1,0:T(8,128)S(1)} %get-tuple-element.24.refs_0_), channel_id=1, source_target_pairs={{0,3},{1,2},{2,1},{3,0},{4,7},{5,6},{6,5},{7,4},{8,11},{9,10},{10,... | collective-permute-start | bytes 12296 | tf_op jit(solution)/shard_map/ppermute | solution.py:289
  12.6 3.7 %collective-permute-start.4 = (s32[8,128]{1,0:T(8,128)S(1)}, s32[8,128]{1,0:T(8,128)S(1)}, u32[]{:S(2)}, u32[]{:S(2)}) collective-permute-start(s32[8,128]{1,0:T(8,128)S(1)} %get-tuple-element.24.refs_0_), channel_id=1, source_target_pairs={{0,2},{1,3},{2,0},{3,1},{4,6},{5,7},{6,4},{7,5},{8,10},{9,11},{10,... | collective-permute-start | bytes 12296 | tf_op jit(solution)/shard_map/ppermute | solution.py:289
  13.0 3.6 %collective-permute-start.5 = (s32[8,128]{1,0:T(8,128)S(1)}, s32[8,128]{1,0:T(8,128)S(1)}, u32[]{:S(2)}, u32[]{:S(2)}) collective-permute-start(s32[8,128]{1,0:T(8,128)S(1)} %get-tuple-element.24.refs_0_), channel_id=1, source_target_pairs={{0,1},{1,0},{2,3},{3,2},{4,5},{5,4},{6,7},{7,6},{8,9},{9,8},{10,11... | collective-permute-start | bytes 12296 | tf_op jit(solution)/shard_map/ppermute | solution.py:289
  13.5 12.2 %collective-permute-start.2 = (bf16[4,144,128]{2,1,0:T(8,128)(2,1)S(1)}, bf16[4,144,128]{2,1,0:T(8,128)(2,1)S(1)}, u32[]{:S(2)}, u32[]{:S(2)}) collective-permute-start(bf16[4,144,128]{2,1,0:T(8,128)(2,1)S(1)} %shard_map.58.refs_4_.refs_3_), channel_id=1, source_target_pairs={{0,4},{1,5},{2,6},{3,7},{4,0},{5,1},{6,2},{7,3},{8,12},{9,13},{10,... | collective-permute-start | bytes 442376 | tf_op jit(solution)/shard_map/ppermute | solution.py:289
  17.5 12.0 %collective-permute-start.6 = (bf16[2,144,384]{2,1,0:T(8,128)(2,1)S(1)}, bf16[2,144,384]{2,1,0:T(8,128)(2,1)S(1)}, u32[]{:S(2)}, u32[]{:S(2)}) collective-permute-start(bf16[2,144,384]{2,1,0:T(8,128)(2,1)S(1)} %get-tuple-element.25), channel_id=1, source_target_pairs={{0,3},{1,2},{2,1},{3,0},{4,7},{5,6},{6,5},{7,4},{8,11},{9,10},{10,... | collective-permute-start | bytes 663560 | tf_op jit(solution)/shard_map/ppermute | solution.py:289
  19.1 13.8 %collective-permute-start.7 = (bf16[2,144,384]{2,1,0:T(8,128)(2,1)S(1)}, bf16[2,144,384]{2,1,0:T(8,128)(2,1)S(1)}, u32[]{:S(2)}, u32[]{:S(2)}) collective-permute-start(bf16[2,144,384]{2,1,0:T(8,128)(2,1)S(1)} %get-tuple-element.26), channel_id=1, source_target_pairs={{0,2},{1,3},{2,0},{3,1},{4,6},{5,7},{6,4},{7,5},{8,10},{9,11},{10,... | collective-permute-start | bytes 663560 | tf_op jit(solution)/shard_map/ppermute | solution.py:289
  20.4 12.6 %collective-permute-start.8 = (bf16[2,144,384]{2,1,0:T(8,128)(2,1)S(1)}, bf16[2,144,384]{2,1,0:T(8,128)(2,1)S(1)}, u32[]{:S(2)}, u32[]{:S(2)}) collective-permute-start(bf16[2,144,384]{2,1,0:T(8,128)(2,1)S(1)} %get-tuple-element.27), channel_id=1, source_target_pairs={{0,1},{1,0},{2,3},{3,2},{4,5},{5,4},{6,7},{7,6},{8,9},{9,8},{10,11... | collective-permute-start | bytes 663560 | tf_op jit(solution)/shard_map/ppermute | solution.py:289
  26.6 8.0 %collective-permute-start.9 = (bf16[2,144,128]{2,1,0:T(8,128)(2,1)S(1)}, bf16[2,144,128]{2,1,0:T(8,128)(2,1)S(1)}, u32[]{:S(2)}, u32[]{:S(2)}) collective-permute-start(bf16[2,144,128]{2,1,0:T(8,128)(2,1)S(1)} %get-tuple-element.28), channel_id=1, source_target_pairs={{0,3},{1,2},{2,1},{3,0},{4,7},{5,6},{6,5},{7,4},{8,11},{9,10},{10,... | collective-permute-start | bytes 221192 | tf_op jit(solution)/shard_map/ppermute | solution.py:289
  28.2 8.0 %collective-permute-start.10 = (bf16[2,144,128]{2,1,0:T(8,128)(2,1)S(1)}, bf16[2,144,128]{2,1,0:T(8,128)(2,1)S(1)}, u32[]{:S(2)}, u32[]{:S(2)}) collective-permute-start(bf16[2,144,128]{2,1,0:T(8,128)(2,1)S(1)} %get-tuple-element.29), channel_id=1, source_target_pairs={{0,2},{1,3},{2,0},{3,1},{4,6},{5,7},{6,4},{7,5},{8,10},{9,11},{10,... | collective-permute-start | bytes 221192 | tf_op jit(solution)/shard_map/ppermute | solution.py:289
  29.5 6.7 %collective-permute-start.11 = (bf16[2,144,128]{2,1,0:T(8,128)(2,1)S(1)}, bf16[2,144,128]{2,1,0:T(8,128)(2,1)S(1)}, u32[]{:S(2)}, u32[]{:S(2)}) collective-permute-start(bf16[2,144,128]{2,1,0:T(8,128)(2,1)S(1)} %get-tuple-element.30), channel_id=1, source_target_pairs={{0,1},{1,0},{2,3},{3,2},{4,5},{5,4},{6,7},{7,6},{8,9},{9,8},{10,11... | collective-permute-start | bytes 221192 | tf_op jit(solution)/shard_map/ppermute | solution.py:289
